TPU v7x, 32 devices: a whole 2x2x4 slice. The times are simulated.
32 devices in a mesh: dp: 2 (over y), dom: 4 (over z), tensor: 4 (over x, core).
Axes of the slice: x: 2, y: 2, z: 4, core: 2. Of those that a mesh axis runs over, the one named last changes fastest.
Arguments:
- states: bfloat16 [2, 2048, 512], P('dp', 'dom'), may hold values from -60 to 60, as said below
- w_query: bfloat16 [512, 512], P(None, 'tensor'), as said below
- w_key: bfloat16 [512, 512], P(None, 'tensor'), as said below
- w_value: bfloat16 [512, 512], P(None, 'tensor'), may hold values from -0.25 to 0.25
- w_out: bfloat16 [512, 512], P('tensor'), may hold values from -0.25 to 0.25
- send_blocks: int32 [4, 4, 2], P('dom'), may hold values from 0 to 3
- neighbor_blocks: int32 [16, 3], P('dom'), may hold values from 0 to 11, as said below
- cotangent: bfloat16 [2, 2048, 512], P('dp', 'dom'), may hold values from -6 to 6
Outputs:
- update: bfloat16 [2, 2048, 512], P('dp', 'dom', 'tensor')
- branch_grad: bfloat16 [2, 2048, 512], P('dp', 'dom', 'tensor')
- grad_query: float32 [512, 512], P(None, 'tensor')
- grad_key: float32 [512, 512], P(None, 'tensor')
- grad_value: float32 [512, 512], P(None, 'tensor')
- grad_out: float32 [512, 512], P('tensor')
Inputs may be any that keep to these rules, and one draw needn't show every extreme that they name: `neighbor_blocks`: entries index the pool of the row's own partition; every pool entry from 4 on is named by some row of that partition. `states`: real entries. `w_query`: real entries. `w_key`: real entries.
All inputs are finite; a program needn't handle non-finite values.
Results may differ from a plain program's by a relative error of at most 0.02.
The roundings to bfloat16 on the way count: a program that leaves them out, or rounds other values in their place, can miss the bound.
Values may be sent and summed in bfloat16 or wider, within the bound.
No kernel may reach another device: no remote copies, remote signals or barrier semaphores. Data moves between devices by JAX's collectives and lax.ppermute only.
A program may use at most 64 MiB of HBM per device.

v0:
```python
import functools
import math

import jax
import jax.numpy as jnp
from jax import lax
from jax.experimental import pallas as pl
from jax.experimental.pallas import tpu as pltpu
from jax.sharding import PartitionSpec as P

BLK = 128
HOPS = 2
SEND = 2
HD = 64
PAD = 16
EARLY = 2
EPS = 1e-05
LIMIT = 24 * 1024 * 1024
SMALL = 8 * 1024 * 1024
CHUNK = 64
BRIEF = pl.CostEstimate(flops=1, bytes_accessed=1, transcendentals=0)
F32 = jnp.float32
BF16 = jnp.bfloat16


def offset_list(hops):
    result = []
    for section in range(1, hops + 1):
        result.append(section)
        result.append(-section)
    return result


def piece_order(ranks, offsets):
    count = offsets * SEND
    share = count // ranks
    if share == SEND and offsets == 4:
        return [0, 1, 4, 5, 2, 3, 6, 7], share
    return list(range(count)), share


def nt(left, right):
    return lax.dot_general(left, right, (((1,), (1,)), ((), ())), preferred_element_type=F32)


def nn(left, right):
    return jnp.dot(left, right, preferred_element_type=F32)


def unit_of(rows):
    values = rows.astype(F32)
    return (values * lax.rsqrt(jnp.mean(values * values, axis=-1, keepdims=True) + EPS)).astype(BF16)


def block_at(index, size=BLK):
    return pl.ds(pl.multiple_of(index * size, size), size)


def rank_piece(rank, ranks, share, inner):
    if share == SEND and ranks == 4:
        return ((rank & 1) * 2 + (rank >> 1)) * SEND + inner
    return rank * share + inner


def in_hbm(*arrays):
    return [pltpu.with_memory_space_constraint(array, pltpu.HBM) for array in arrays]


def pick_kernel(ranks, share, send_ref, states_ref, *refs):
    outs, table, sems = refs[:share], refs[share], refs[share + 1]
    rank = lax.axis_index("tensor")
    fetch = pltpu.make_async_copy(send_ref, table, sems.at[share])
    fetch.start()
    fetch.wait()
    copies = []
    for inner, out_ref in enumerate(outs):
        piece = rank_piece(rank, ranks, share, inner)
        block = table[piece % SEND, piece // SEND]
        copies.append(
            pltpu.make_async_copy(states_ref.at[block_at(block), :], out_ref, sems.at[inner])
        )
        copies[-1].start()
    for copy in copies:
        copy.wait()


def pick_blocks(states, send, ranks, share):
    far = pl.BlockSpec(memory_space=pltpu.HBM)
    vmem = pl.BlockSpec(memory_space=pltpu.VMEM)
    return pl.pallas_call(
        functools.partial(pick_kernel, ranks, share),
        out_shape=[jax.ShapeDtypeStruct((BLK, states.shape[1]), BF16)] * share,
        in_specs=[far, far],
        out_specs=[vmem] * share,
        scratch_shapes=[
            pltpu.SMEM(send.shape, jnp.int32),
            pltpu.SemaphoreType.DMA((share + 1,)),
        ],
        compiler_params=pltpu.CompilerParams(vmem_limit_bytes=SMALL),
        cost_estimate=BRIEF,
        name="pick_blocks",
    )(*in_hbm(send, states))


def by_head(rows, heads):
    if heads == 1:
        return rows.astype(BF16)
    lane_head = lax.broadcasted_iota(jnp.int32, rows.shape, 1) // HD
    return jnp.concatenate(
        [jnp.where(lane_head == head, rows, 0.0) for head in range(heads)], axis=0
    ).astype(BF16)


def diagonal(stacked, heads):
    return jnp.concatenate(
        [
            stacked[head * HD : (head + 1) * HD, head * BLK : (head + 1) * BLK]
            for head in range(heads)
        ],
        axis=0,
    )


def put_pairs(paired, at, width, k_ref, v_ref, kt_ref, vt_ref):
    for index, entry in enumerate(at):
        rows = paired[index * BLK : (index + 1) * BLK]
        keys, values = rows[:, :width], rows[:, width:]
        k_ref[block_at(entry), :] = keys.astype(BF16)
        v_ref[block_at(entry), :] = values.astype(BF16)
        kt_ref[entry] = keys.T.astype(BF16)
        vt_ref[entry] = values.T.astype(BF16)


def own_kernel(*refs):
    sources = refs[:6]
    unit_ref, q_ref, g_ref, k_ref, v_ref, kt_ref, vt_ref, slab_ref, inverse_ref = refs[6:15]
    held, states_ref, sems = refs[15:20], refs[20], refs[21]
    cot_ref, wq_ref, wk_ref, wv_ref, wo_ref = held
    copies = []
    for index, (source, target) in enumerate(zip(sources, (states_ref,) + tuple(held))):
        copies.append(pltpu.make_async_copy(source, target, sems.at[index]))
        copies[-1].start()
    rows, feats = states_ref.shape
    width = wq_ref.shape[1]
    heads = width // HD
    tall = heads * BLK
    rank = lax.axis_index("tensor")
    copies[0].wait()
    for start in range(0, rows, CHUNK):
        values = states_ref[start : start + CHUNK, :].astype(F32)
        inverse = lax.rsqrt(jnp.mean(values * values, axis=-1, keepdims=True) + EPS)
        normed = values * inverse
        unit_ref[start : start + CHUNK, :] = normed.astype(BF16)
        slab = normed[:, :width]
        for index in range(1, feats // width):
            slab = jnp.where(rank == index, normed[:, index * width : (index + 1) * width], slab)
        slab_ref[start : start + CHUNK, :] = slab
        inverse_ref[start : start + CHUNK, :] = jnp.broadcast_to(inverse, slab.shape)
    for copy in copies[1:]:
        copy.wait()
    unit = unit_ref[...]
    queries = nn(unit, wq_ref[...])
    grads = nt(cot_ref[...], wo_ref[...])
    for block in range(rows // BLK):
        q_ref[block * tall : (block + 1) * tall, :] = by_head(
            queries[block * BLK : (block + 1) * BLK], heads
        )
        g_ref[block * tall : (block + 1) * tall, :] = by_head(
            grads[block * BLK : (block + 1) * BLK], heads
        )
    paired = nn(unit, jnp.concatenate([wk_ref[...], wv_ref[...]], axis=1))
    put_pairs(paired, range(rows // BLK), width, k_ref, v_ref, kt_ref, vt_ref)


def run_own(states, cot, weights):
    rows, feats = states.shape
    width = weights[0].shape[1]
    blocks = rows // BLK
    tall = blocks * (width // HD) * BLK
    vmem = pl.BlockSpec(memory_space=pltpu.VMEM)
    far = pl.BlockSpec(memory_space=pltpu.HBM)
    shape = jax.ShapeDtypeStruct
    return pl.pallas_call(
        own_kernel,
        out_shape=(
            shape((rows, feats), BF16),
            shape((tall, width), BF16),
            shape((tall, width), BF16),
            shape((rows, width), BF16),
            shape((rows, width), BF16),
            shape((blocks, width, BLK), BF16),
            shape((blocks, width, BLK), BF16),
            shape((rows, width), F32),
            shape((rows, width), F32),
            shape(cot.shape, BF16),
            *[shape(w.shape, BF16) for w in weights],
        ),
        in_specs=[far] * 6,
        out_specs=[vmem] * 14,
        scratch_shapes=[pltpu.VMEM((rows, feats), BF16), pltpu.SemaphoreType.DMA((6,))],
        compiler_params=pltpu.CompilerParams(vmem_limit_bytes=LIMIT),
        cost_estimate=BRIEF,
        name="own_rows",
    )(*in_hbm(states, cot, *weights))


def early_kernel(count, *refs):
    piece_refs, (wk_ref, wv_ref) = refs[:count], refs[count : count + 2]
    unit_ref, k_ref, v_ref, kt_ref, vt_ref = refs[count + 2 :]
    width = wk_ref.shape[1]
    at = 0
    for source in piece_refs:
        for start in range(0, source.shape[0], CHUNK):
            unit_ref[at : at + CHUNK, :] = unit_of(source[start : start + CHUNK, :])
            at += CHUNK
    wkv = jnp.concatenate([wk_ref[...], wv_ref[...]], axis=1)
    paired = nn(unit_ref[...], wkv)
    blocks = range(unit_ref.shape[0] // BLK)
    put_pairs(paired, blocks, width, k_ref, v_ref, kt_ref, vt_ref)


def run_early(pieces, w_key, w_value):
    inputs, count = len(pieces), sum(piece.shape[0] for piece in pieces) // BLK
    feats, width = w_key.shape
    vmem = pl.BlockSpec(memory_space=pltpu.VMEM)
    shape = jax.ShapeDtypeStruct
    return pl.pallas_call(
        functools.partial(early_kernel, inputs),
        out_shape=(
            shape((count * BLK, feats), BF16),
            shape((count * BLK, width), BF16),
            shape((count * BLK, width), BF16),
            shape((count, width, BLK), BF16),
            shape((count, width, BLK), BF16),
        ),
        in_specs=[vmem] * (inputs + 2),
        out_specs=[vmem] * 5,
        compiler_params=pltpu.CompilerParams(vmem_limit_bytes=LIMIT),
        cost_estimate=BRIEF,
        name="early_rows",
    )(*pieces, w_key, w_value)


def attend_kernel(cfg, near_ref, *refs):
    ranks, share, blocks, offsets, width, explicit, early = cfg
    early_refs, refs = refs[:5], refs[5:]
    count = (ranks - early) * share
    piece_refs = refs[:count]
    own_refs = refs[count : count + 7]
    cot_ref, wk_ref, wv_ref = refs[count + 7 : count + 10]
    refs = refs[count + 10 :]
    both_ref, dq_ref, mixed_ref = refs[:3]
    far_refs, half_refs = refs[3:5], refs[5:9]
    pool_ref, refs = refs[9], refs[10:]
    k_ref, v_ref, kt_ref, vt_ref, ka_ref, va_ref, dk_ref, dv_ref = refs[:8]
    score_ref, prob_ref, low_ref, change_ref, near_table, near_sem = refs[8:]
    fetch = pltpu.make_async_copy(near_ref, near_table, near_sem)
    fetch.start()
    q_ref, g_ref, k_own, v_own, kt_own, vt_own = own_refs[1:]
    heads = width // HD
    tall = heads * BLK
    entries = blocks + offsets * SEND
    rank = lax.axis_index("tensor")

    own_rows = blocks * BLK
    k_ref[:own_rows, :] = k_own[...]
    v_ref[:own_rows, :] = v_own[...]
    kt_ref[:blocks] = kt_own[...]
    vt_ref[:blocks] = vt_own[...]
    wkv = jnp.concatenate([wk_ref[...], wv_ref[...]], axis=1)
    unit_e, k_e, v_e, kt_e, vt_e = early_refs
    for slot in range(early):
        for inner in range(share):
            entry = rank_piece(rank ^ slot, ranks, share, inner)
            index = slot * share + inner
            rows = slice(index * BLK, (index + 1) * BLK)
            pool_ref[block_at(entry), :] = unit_e[rows, :]
            k_ref[block_at(entry + blocks), :] = k_e[rows, :]
            v_ref[block_at(entry + blocks), :] = v_e[rows, :]
            kt_ref[entry + blocks] = kt_e[index]
            vt_ref[entry + blocks] = vt_e[index]
    late, places = [], []
    for slot in range(early, ranks):
        for inner in range(share):
            entry = rank_piece(rank ^ slot, ranks, share, inner)
            base = pl.multiple_of(entry * BLK, BLK)
            places.append(entry + blocks)
            source = piece_refs[(slot - early) * share + inner]
            for start in range(0, BLK, CHUNK):
                rows = unit_of(source[start : start + CHUNK, :])
                pool_ref[pl.ds(pl.multiple_of(base + start, CHUNK), CHUNK), :] = rows
                late.append(rows)
    paired = nn(jnp.concatenate(late, axis=0), wkv)
    put_pairs(paired, places, width, k_ref, v_ref, kt_ref, vt_ref)

    shrink = 1.0 / math.sqrt(HD)
    near = near_ref.shape[1]
    fetch.wait()
    listed = [[block] + [near_table[block, n] for n in range(near)] for block in range(blocks)]

    def open_block(block):
        keys = jnp.concatenate([k_ref[block_at(e), :] for e in listed[block]], axis=0)
        values = jnp.concatenate([v_ref[block_at(e), :] for e in listed[block]], axis=0)
        score_ref[block] = nt(keys, q_ref[block * tall : (block + 1) * tall, :]) * shrink
        prob_ref[block] = nt(values, g_ref[block * tall : (block + 1) * tall, :])

    def weigh_block(block):
        spans = [slice(n * CHUNK, (n + 1) * CHUNK) for n in range((near + 1) * BLK // CHUNK)]
        highest = jnp.max(score_ref[block, spans[0], :], axis=0, keepdims=True)
        for span in spans[1:]:
            rows = jnp.max(score_ref[block, span, :], axis=0, keepdims=True)
            highest = jnp.maximum(highest, rows)
        total, drop = jnp.zeros_like(highest), jnp.zeros_like(highest)
        for span in spans:
            powers = jnp.exp(score_ref[block, span, :] - highest)
            score_ref[block, span, :] = powers
            total = total + jnp.sum(powers, axis=0, keepdims=True)
            drop = drop + jnp.sum(powers * prob_ref[block, span, :], axis=0, keepdims=True)
        scale = 1.0 / total
        drop = drop * scale
        for span in spans:
            weights = score_ref[block, span, :] * scale
            low_ref[block, span, :] = weights.astype(BF16)
            change = weights * (prob_ref[block, span, :] - drop) * shrink
            change_ref[block, span, :] = change.astype(BF16)

    def close_block(block):
        rows = slice(block * BLK, (block + 1) * BLK)
        keys_t = jnp.concatenate([kt_ref[e] for e in listed[block]], axis=1)
        values_t = jnp.concatenate([vt_ref[e] for e in listed[block]], axis=1)
        low, change = low_ref[block], change_ref[block]
        mixed_ref[rows, :] = diagonal(nn(values_t, low), heads).T.astype(BF16)
        dq_ref[rows, :] = diagonal(nn(keys_t, change), heads).T.astype(BF16)
        dk = nn(change, q_ref[block * tall : (block + 1) * tall, :])
        dv = nn(low, g_ref[block * tall : (block + 1) * tall, :])
        ka_ref[rows, :] = dk[:BLK]
        va_ref[rows, :] = dv[:BLK]
        dk_ref[block] = dk[BLK:]
        dv_ref[block] = dv[BLK:]

    open_block(0)
    for block in range(blocks):
        if block + 1 < blocks:
            open_block(block + 1)
        weigh_block(block)
        if block:
            close_block(block - 1)
    close_block(blocks - 1)

    ka_ref[own_rows:, :] = jnp.zeros((entries * BLK - own_rows, width), F32)
    va_ref[own_rows:, :] = jnp.zeros((entries * BLK - own_rows, width), F32)
    for block in range(blocks):
        for n in range(near):
            entry = block_at(listed[block][n + 1])
            ka_ref[entry, :] += dk_ref[block, n * BLK : (n + 1) * BLK]
            va_ref[entry, :] += dv_ref[block, n * BLK : (n + 1) * BLK]

    both_ref[:, :width] = ka_ref[...].astype(BF16)
    both_ref[:, width:] = va_ref[...].astype(BF16)
    grad_terms(explicit, own_refs[0], pool_ref, both_ref, dq_ref, mixed_ref, cot_ref, *half_refs)
    far_terms(blocks, pool_ref, both_ref, wk_ref, wv_ref, *far_refs)


def grad_terms(explicit, unit_ref, pool_ref, both_ref, dq_ref, mixed_ref, cot_ref, *refs):
    first_keep, first_send, second_keep, second_send = refs
    rows, width = dq_ref.shape

    def turned(ref, first, last):
        parts = [
            ref[start : start + BLK, :].astype(F32).T.astype(BF16)
            for start in range(first, last, BLK)
        ]
        return jnp.concatenate(parts, axis=1)

    unit = unit_ref[...]
    grad_q = nn(turned(dq_ref, 0, rows), unit)
    grad_out = nn(turned(mixed_ref, 0, rows), cot_ref[...])
    grad_kv = nn(turned(both_ref, 0, rows), unit)
    grad_kv = grad_kv + nn(turned(both_ref, rows, both_ref.shape[0]), pool_ref[...])
    grad_k, grad_v = grad_kv[:width], grad_kv[width:]
    by_dp = jnp.equal(lax.axis_index("dp") if explicit else 0, 1)
    by_dom = jnp.equal(lax.axis_index("dom") & 1 if explicit else 0, 1)
    first_keep[...] = jnp.where(by_dp, grad_k, grad_q).astype(BF16)
    first_send[...] = jnp.where(by_dp, grad_q, grad_k).astype(BF16)
    second_keep[...] = jnp.where(by_dom, grad_out, grad_v).astype(BF16)
    second_send[...] = jnp.where(by_dom, grad_v, grad_out).astype(BF16)


def run_attend(explicit, early, ranks, share, offsets, near, pieces, own, cot, w_key, w_value):
    rows, feats = own[0].shape
    blocks = rows // BLK
    width = w_key.shape[1]
    received = offsets * SEND
    entries = blocks + received
    listed, tall = (near.shape[1] + 1) * BLK, width // HD * BLK
    vmem = pl.BlockSpec(memory_space=pltpu.VMEM)
    far = pl.BlockSpec(memory_space=pltpu.HBM)
    cfg = (ranks, share, blocks, offsets, width, explicit, EARLY)
    shape = jax.ShapeDtypeStruct
    return pl.pallas_call(
        functools.partial(attend_kernel, cfg),
        out_shape=[
            shape((entries * BLK, 2 * width), BF16),
            shape((rows, width), BF16),
            shape((rows, width), BF16),
            *[shape((feats // width // 2, offsets * (SEND * BLK + PAD), width), BF16)] * 2,
            *[shape((width, feats), BF16)] * 4,
        ],
        in_specs=[far] + [vmem] * (len(early) + len(pieces) + 10),
        out_specs=[vmem] * 9,
        scratch_shapes=[
            pltpu.VMEM((received * BLK, feats), BF16),
            pltpu.VMEM((entries * BLK, width), BF16),
            pltpu.VMEM((entries * BLK, width), BF16),
            pltpu.VMEM((entries, width, BLK), BF16),
            pltpu.VMEM((entries, width, BLK), BF16),
            pltpu.VMEM((entries * BLK, width), F32),
            pltpu.VMEM((entries * BLK, width), F32),
            pltpu.VMEM((blocks, near.shape[1] * BLK, width), F32),
            pltpu.VMEM((blocks, near.shape[1] * BLK, width), F32),
            *[pltpu.VMEM((blocks, listed, tall), F32)] * 2,
            *[pltpu.VMEM((blocks, listed, tall), BF16)] * 2,
            pltpu.SMEM(near.shape, jnp.int32),
            pltpu.SemaphoreType.DMA(()),
        ],
        compiler_params=pltpu.CompilerParams(vmem_limit_bytes=LIMIT),
        cost_estimate=BRIEF,
        name="attention",
    )(*in_hbm(near), *early, *pieces, *own, cot, w_key, w_value)


def put(odd, upper, keep_ref, send_ref, row, values):
    count, width = values.shape[0], keep_ref.shape[2]
    for pair in range(values.shape[1] // width // 2):
        left = values[:, 2 * pair * width : (2 * pair + 1) * width]
        right = values[:, (2 * pair + 1) * width : (2 * pair + 2) * width]
        at = upper ^ pair
        keep_ref[at, row : row + count, :] = jnp.where(odd, right, left).astype(BF16)
        send_ref[at, row : row + count, :] = jnp.where(odd, left, right).astype(BF16)


def put_dots(keep_ref, send_ref, row, dots):
    width = keep_ref.shape[2]
    parts = []
    for dot in dots:
        for piece in range(BLK // width):
            parts.append(dot[:1, piece * width : (piece + 1) * width])
    parts.append(jnp.zeros((PAD - len(parts), width), F32))
    rows = jnp.concatenate(parts, axis=0).astype(BF16)
    for pair in range(keep_ref.shape[0]):
        keep_ref[pair, row : row + PAD, :] = rows
        send_ref[pair, row : row + PAD, :] = rows


def row_dot(term, ref, first):
    ones = jnp.ones((16, ref.shape[1]), BF16)
    product = (term * ref[first : first + BLK, :].astype(F32)).astype(BF16)
    return nt(ones, product)


def far_terms(blocks, pool_ref, both_ref, wk_ref, wv_ref, far_keep, far_send):
    rank = lax.axis_index("tensor")
    odd, upper = (rank & 1) == 1, rank >> 1
    rows, step = blocks * BLK, SEND * BLK
    wkv = jnp.concatenate([wk_ref[...], wv_ref[...]], axis=1)
    for index in range(pool_ref.shape[0] // step):
        first, at = index * step, index * (step + PAD)
        term = nt(both_ref[rows + first : rows + first + step, :], wkv)
        put(odd, upper, far_keep, far_send, at, term)
        dots = [
            row_dot(term[c * BLK : (c + 1) * BLK], pool_ref, first + c * BLK) for c in range(SEND)
        ]
        put_dots(far_keep, far_send, at + step, dots)


def own_terms_kernel(both_ref, unit_ref, dq_ref, mixed_ref, *refs):
    wq_ref, wk_ref, wv_ref, wo_ref, own_keep, own_send = refs
    rank = lax.axis_index("tensor")
    odd, upper = (rank & 1) == 1, rank >> 1
    rows, step = unit_ref.shape[0], 2 * BLK
    wkv = jnp.concatenate([wk_ref[...], wv_ref[...]], axis=1)
    dots = []
    for first in range(0, rows, step):
        last = first + step
        term = nt(both_ref[first:last, :], wkv) + nt(dq_ref[first:last, :], wq_ref[...])
        put(odd, upper, own_keep, own_send, first, term)
        dots += [row_dot(term[c * BLK : (c + 1) * BLK], unit_ref, first + c * BLK) for c in (0, 1)]
        update = nn(mixed_ref[first:last, :], wo_ref[...])
        put(odd, upper, own_keep, own_send, rows + PAD + first, update)
    put_dots(own_keep, own_send, rows, dots)


def run_own_terms(both, unit, dq, mixed, weights):
    rows, feats = unit.shape
    width = dq.shape[1]
    vmem = pl.BlockSpec(memory_space=pltpu.VMEM)
    own = jax.ShapeDtypeStruct((feats // width // 2, 2 * rows + PAD, width), BF16)
    return pl.pallas_call(
        own_terms_kernel,
        out_shape=(own, own),
        in_specs=[vmem] * 8,
        out_specs=[vmem] * 2,
        compiler_params=pltpu.CompilerParams(vmem_limit_bytes=LIMIT),
        cost_estimate=BRIEF,
        name="own_terms",
    )(both, unit, dq, mixed, *weights)


def returns_kernel(bounds, keep_ref, got_ref, last_ref, *outs):
    for (first, last), out_ref in zip(bounds, outs):
        total = keep_ref[0, first:last, :].astype(F32) + got_ref[0, first:last, :].astype(F32)
        out_ref[...] = (total + last_ref[first:last, :].astype(F32)).astype(BF16)


def run_returns(bounds, keep, got, last):
    vmem = pl.BlockSpec(memory_space=pltpu.VMEM)
    width = keep.shape[2]
    return pl.pallas_call(
        functools.partial(returns_kernel, bounds),
        out_shape=[jax.ShapeDtypeStruct((b - a, width), BF16) for a, b in bounds],
        in_specs=[vmem] * 3,
        out_specs=[vmem] * len(bounds),
        compiler_params=pltpu.CompilerParams(vmem_limit_bytes=SMALL),
        cost_estimate=BRIEF,
        name="returned_terms",
    )(keep, got, last)


def my_bits():
    dom = lax.axis_index("dom")
    return lax.axis_index("dp"), dom & 1, dom >> 1


def halve_kernel(bits, *refs):
    count = len(bits)
    ins, outs = refs[: 2 * count], refs[2 * count :]
    mine = my_bits()
    size = outs[0].shape[0]
    for index, bit in enumerate(bits):
        keep_ref, got_ref = ins[2 * index : 2 * index + 2]
        for side, name in enumerate((mine[bit], 1 - mine[bit])):
            at = block_at(name, size)
            total = keep_ref[at, :].astype(F32) + got_ref[at, :].astype(F32)
            outs[2 * index + side][...] = total.astype(BF16)


def run_halve(bits, *arrays):
    vmem = pl.BlockSpec(memory_space=pltpu.VMEM)
    rows, feats = arrays[0].shape
    return pl.pallas_call(
        functools.partial(halve_kernel, bits),
        out_shape=[jax.ShapeDtypeStruct((rows // 2, feats), BF16)] * len(arrays),
        in_specs=[vmem] * len(arrays),
        out_specs=[vmem] * len(arrays),
        compiler_params=pltpu.CompilerParams(vmem_limit_bytes=SMALL),
        cost_estimate=BRIEF,
        name="halve_grads",
    )(*arrays)


def total_kernel(*refs):
    out_ref = refs[-1]
    size = refs[0].shape[0]
    for index in range(len(refs) // 2):
        total = refs[2 * index][...].astype(F32) + refs[2 * index + 1][...].astype(F32)
        out_ref[index * size : (index + 1) * size, :] = total.astype(BF16)


def run_total(*arrays):
    vmem = pl.BlockSpec(memory_space=pltpu.VMEM)
    rows, feats = arrays[0].shape
    return pl.pallas_call(
        total_kernel,
        out_shape=jax.ShapeDtypeStruct((len(arrays) // 2 * rows, feats), BF16),
        in_specs=[vmem] * len(arrays),
        out_specs=vmem,
        compiler_params=pltpu.CompilerParams(vmem_limit_bytes=SMALL),
        cost_estimate=BRIEF,
        name="total_grads",
    )(*arrays)


def settle_kernel(mine_ref, got_ref, *outs):
    size = outs[0].shape[0]
    for index, out_ref in enumerate(outs):
        rows = slice(index * size, (index + 1) * size)
        total = mine_ref[rows, :].astype(F32) + got_ref[rows, :].astype(F32)
        out_ref[...] = total.astype(BF16)


def run_settle(mine, got):
    vmem = pl.BlockSpec(memory_space=pltpu.VMEM)
    rows, feats = mine.shape
    return pl.pallas_call(
        settle_kernel,
        out_shape=[jax.ShapeDtypeStruct((rows // 2, feats), BF16)] * 2,
        in_specs=[vmem] * 2,
        out_specs=[vmem] * 2,
        compiler_params=pltpu.CompilerParams(vmem_limit_bytes=SMALL),
        cost_estimate=BRIEF,
        name="settle_grads",
    )(mine, got)


def join_kernel(bits, *refs):
    count = len(bits)
    outs = refs[-count:]
    mine = my_bits()
    size = refs[0].shape[0]
    for index, bit in enumerate(bits):
        outs[index][block_at(mine[bit], size), :] = refs[2 * index][...]
        outs[index][block_at(1 - mine[bit], size), :] = refs[2 * index + 1][...]


def run_join(bits, *arrays):
    vmem = pl.BlockSpec(memory_space=pltpu.VMEM)
    rows, feats = arrays[0].shape
    return pl.pallas_call(
        functools.partial(join_kernel, bits),
        out_shape=[jax.ShapeDtypeStruct((2 * rows, feats), BF16)] * len(bits),
        in_specs=[vmem] * len(arrays),
        out_specs=[vmem] * len(bits),
        compiler_params=pltpu.CompilerParams(vmem_limit_bytes=SMALL),
        cost_estimate=BRIEF,
        name="join_grads",
    )(*arrays)


def own_sum_kernel(keep_ref, got_ref, last_ref, update_ref, unit_ref):
    rows = update_ref.shape[0]

    def total(first, last):
        both = keep_ref[0, first:last, :].astype(F32) + got_ref[0, first:last, :].astype(F32)
        return both + last_ref[first:last, :].astype(F32)

    unit_ref[...] = total(0, rows + PAD)
    update_ref[...] = total(rows + PAD, 2 * rows + PAD).astype(BF16)


def run_own_sum(rows, keep, got, last):
    width = last.shape[1]
    vmem = pl.BlockSpec(memory_space=pltpu.VMEM)
    shape = jax.ShapeDtypeStruct
    return pl.pallas_call(
        own_sum_kernel,
        out_shape=(shape((rows, width), BF16), shape((rows + PAD, width), F32)),
        in_specs=[vmem] * 3,
        out_specs=[vmem] * 2,
        compiler_params=pltpu.CompilerParams(vmem_limit_bytes=SMALL),
        cost_estimate=BRIEF,
        name="own_sum",
    )(keep, got, last)


def finish_kernel(cfg, *refs):
    blocks, offsets, width, feats, spread = cfg
    send_ref, sum_ref, slab_ref, inverse_ref = refs[:4]
    far_refs = refs[4 : 4 + len(spread)]
    branch_ref, unit_ref, table, sem = refs[4 + len(spread) :]
    fetch = pltpu.make_async_copy(send_ref, table, sem)
    fetch.start()
    own_rows = blocks * BLK
    sub = BLK // width
    group = SEND * BLK + PAD

    unit_ref[...] = sum_ref[:own_rows, :]
    dots = sum_ref[own_rows:, :]
    at_row = lax.broadcasted_iota(jnp.int32, (PAD, width), 0)
    fetch.wait()
    for ref, members in zip(far_refs, spread):
        for position, offset in enumerate(members):
            first = position * group
            extra = ref[first + SEND * BLK : first + group, :].astype(F32)
            for c in range(SEND):
                block = table[c, offset]
                rows = ref[first + c * BLK : first + (c + 1) * BLK, :].astype(F32)
                unit_ref[block_at(block), :] += rows
                for piece in range(sub):
                    line = extra[c * sub + piece : c * sub + piece + 1, :]
                    dots = dots + jnp.where(at_row == block * sub + piece, line, 0.0)
    for block in range(blocks):
        rows = slice(block * BLK, (block + 1) * BLK)
        line = jnp.concatenate(
            [dots[block * sub + piece : block * sub + piece + 1, :] for piece in range(sub)], axis=1
        )
        mean = jnp.broadcast_to(line * (1.0 / feats), (BLK, BLK)).T[:, :width]
        branch = inverse_ref[rows, :] * (unit_ref[rows, :] - slab_ref[rows, :] * mean)
        branch_ref[rows, :] = branch.astype(BF16)


def run_finish(feats, send, own_sum, slab, inverse, far, spread):
    rows, width = slab.shape
    vmem = pl.BlockSpec(memory_space=pltpu.VMEM)
    hbm = pl.BlockSpec(memory_space=pltpu.HBM)
    cfg = (rows // BLK, send.shape[1], width, feats, spread)
    return pl.pallas_call(
        functools.partial(finish_kernel, cfg),
        out_shape=jax.ShapeDtypeStruct((rows, width), BF16),
        in_specs=[hbm] + [vmem] * (3 + len(far)),
        out_specs=vmem,
        scratch_shapes=[
            pltpu.VMEM((rows, width), F32),
            pltpu.SMEM(send.shape, jnp.int32),
            pltpu.SemaphoreType.DMA(()),
        ],
        compiler_params=pltpu.CompilerParams(vmem_limit_bytes=SMALL),
        cost_estimate=BRIEF,
        name="finish",
    )(*in_hbm(send), own_sum, slab, inverse, *far)


def grads_kernel(factor, *refs):
    first_held, first_got, second_held, second_got, q_ref, k_ref, v_ref, o_ref = refs
    dp, low, _ = my_bits()
    first, second = jnp.equal(dp, 1), jnp.equal(low, 1)

    def picked(flag, left, right, start):
        columns = slice(start, start + BLK)
        return jnp.where(flag, left[:, columns].astype(F32), right[:, columns].astype(F32)) * factor

    for start in range(0, q_ref.shape[0], BLK):
        rows = slice(start, start + BLK)
        q_ref[rows, :] = picked(first, first_got, first_held, start).T
        k_ref[rows, :] = picked(first, first_held, first_got, start).T
        v_ref[rows, :] = picked(second, second_got, second_held, start).T
        o_ref[:, rows] = picked(second, second_held, second_got, start)


def run_grads(factor, *arrays):
    width, feats = arrays[0].shape
    vmem = pl.BlockSpec(memory_space=pltpu.VMEM)
    tall = jax.ShapeDtypeStruct((feats, width), F32)
    return pl.pallas_call(
        functools.partial(grads_kernel, factor),
        out_shape=(tall, tall, tall, jax.ShapeDtypeStruct((width, feats), F32)),
        in_specs=[vmem] * 4,
        out_specs=[vmem] * 4,
        compiler_params=pltpu.CompilerParams(vmem_limit_bytes=SMALL),
        cost_estimate=BRIEF,
        name="weight_grads",
    )(*arrays)


def swap(array, axis, bit):
    return lax.ppermute(array, axis, [(i, i ^ bit) for i in range(lax.axis_size(axis))])


def shifted(array, axis, distance):
    size = lax.axis_size(axis)
    return lax.ppermute(array, axis, [(i, (i + distance) % size) for i in range(size)])


def added(left, right):
    return (left.astype(F32) + right.astype(F32)).astype(BF16)


def after(values, *earlier):
    held = lax.optimization_barrier((values, earlier))
    return held[0]


def narrow(keep, got, bit):
    while keep.shape[0] > 2:
        summed = added(keep, got)
        keep, send = summed[0::2], summed[1::2]
        got = swap(send, "tensor", bit)
        bit *= 2
    return keep, got, bit


def body(states, w_query, w_key, w_value, w_out, send_blocks, neighbor_blocks, cotangent):
    replicas, node_count, feats = states.shape
    width = w_query.shape[1]
    ranks = lax.axis_size("tensor")
    parts = lax.axis_size("dom")
    explicit = parts == 4 and lax.axis_size("dp") == 2
    offsets = offset_list(HOPS)
    order, share = piece_order(ranks, len(offsets))
    send = send_blocks[0].T
    weights = (w_query, w_key, w_value, w_out)
    flat_states = states.reshape(-1, feats)
    flat_cot = cotangent.reshape(-1, feats)

    leaving = pick_blocks(flat_states, send, ranks, share)
    route = []
    for p in range(parts):
        for r in range(ranks):
            distance = offsets[order[r * share] // SEND]
            route.append((p * ranks + r, ((p + distance) % parts) * ranks + r))
    levels = []
    bit = 1
    while bit < ranks:
        levels.append(bit)
        bit *= 2
    arrived = [lax.ppermute(block, ("dom", "tensor"), route) for block in leaving]
    own = run_own(flat_states, flat_cot, weights)
    arrived[0] = after(arrived[0], own[0])
    unit, slab, inverse, cot = own[0], own[7], own[8], own[9]
    weights = own[10:]
    first_pieces = list(arrived)
    wide = [swap(block, "tensor", levels[-1]) for block in arrived]
    close = after(first_pieces, *arrived)
    close = [swap(half, "tensor", 1) for block in close for half in jnp.split(block, 2)]
    early = run_early(first_pieces + close, weights[1], weights[2])
    held = {levels[-1]: after(wide, early[0])}
    for bit in reversed(levels[:-1]):
        for slot in list(held):
            held[slot ^ bit] = [swap(block, "tensor", bit) for block in held[slot]]
    for bit in levels[1:-1]:
        held[bit] = [swap(block, "tensor", bit) for block in first_pieces]
        held[bit ^ 1] = [swap(block, "tensor", 1) for block in held[bit]]
    pieces = [block for slot in range(EARLY, ranks) for block in held[slot]]
    count = len(offsets)
    both, dq, mixed, far_keep, far_send, *halves = run_attend(
        explicit,
        early,
        ranks,
        share,
        count,
        neighbor_blocks,
        pieces,
        own[:7],
        cot,
        weights[1],
        weights[2],
    )
    total_rows = replicas * node_count * lax.axis_size("dp") * parts
    factor = 1.0 / math.sqrt(total_rows)

    if explicit:
        first, second = swap(halves[1], "dp", 1), swap(halves[3], "dom", 1)
    far_keep, far_got, bit = narrow(far_keep, swap(far_send, "tensor", 1), 2)
    own_keep, own_send = run_own_terms(both, unit, dq, mixed, weights)
    own_keep, own_got, bit = narrow(own_keep, swap(own_send, "tensor", 1), 2)
    far_out = added(far_keep[1], far_got[1])
    far_last = swap(far_out, "tensor", bit)
    if explicit:
        first, second = after(first, far_out, own_send), after(second, far_out, own_send)
        halves = run_halve((1, 0), halves[0], first, halves[2], second)
        first, second = swap(halves[1], "dom", 1), swap(halves[3], "dp", 1)
        total = run_total(halves[0], first, halves[2], second)
        got = swap(total, "dom", 2)
        own_got = after(own_got, total)
    own_out = added(own_keep[1], own_got[1])
    own_last = swap(own_out, "tensor", bit)
    far_last = after(far_last, own_out)

    group = SEND * BLK + PAD
    spread = []
    for index, distance in enumerate(offsets):
        for members in spread:
            if (offsets[members[0]] - distance) % parts == 0 and members[-1] == index - 1:
                members.append(index)
                break
        else:
            spread.append([index])
    spread = tuple(tuple(members) for members in spread)
    bounds = tuple((members[0] * group, (members[-1] + 1) * group) for members in spread)
    far_sums = run_returns(bounds, far_keep, far_got, far_last)
    returned = [
        shifted(part, "dom", -offsets[members[0]]) for part, members in zip(far_sums, spread)
    ]
    own_last = after(own_last, far_sums)
    update, own_sum = run_own_sum(replicas * node_count, own_keep, own_got, own_last)
    if explicit:
        held = run_settle(total, after(got, own_sum))
        first, second = swap(held[0], "dom", 1), swap(held[1], "dp", 1)
        first = after(first, returned)
        held = run_join((1, 0), held[0], first, held[1], second)
        first, second = swap(held[0], "dp", 1), swap(held[1], "dom", 1)
    branch = run_finish(feats, send, own_sum, slab, inverse, returned, spread)
    if explicit:
        first = after(first, branch)
        grads = run_grads(factor, held[0], first, held[1], second)
    else:
        summed = [lax.psum(half.astype(F32), ("dp", "dom")) * factor for half in halves]
        grads = (summed[0].T, summed[1].T, summed[2].T, summed[3])
    shape = (replicas, node_count, width)
    return (update.reshape(shape), branch.reshape(shape), *grads)


def solution(mesh):
    placed = (
        P("dp", "dom", None),
        P(None, "tensor"),
        P(None, "tensor"),
        P(None, "tensor"),
        P("tensor", None),
        P("dom", None, None),
        P("dom", None),
        P("dp", "dom", None),
    )
    return jax.shard_map(
        body,
        mesh=mesh,
        in_specs=placed,
        out_specs=(
            P("dp", "dom", "tensor"),
            P("dp", "dom", "tensor"),
            P(None, "tensor"),
            P(None, "tensor"),
            P(None, "tensor"),
            P("tensor", None),
        ),
        check_vma=False,
    )
```

profile of v0, /device:TPU:0, one launch (start us, length us, event | category | flops | bytes accessed | tf_op | source)
XLA Modules:
  0.0 66.7 jit_solution(17666220904069672913)
XLA Ops:
  0.6 1.7 %pick_blocks.1 = (bf16[128,512]{1,0:T(8,128)(2,1)S(1)}, bf16[128,512]{1,0:T(8,128)(2,1)S(1)}) custom-call(s32[2,4]{1,0:T(2,128)} %bitcast.15, bf16[512,512]{1,0:T(8,128)(2,1)} %bitcast.11), custom_call_target="tpu_custom_call" | custom-call | flops 1 | bytes 1 | tf_op jit(solution)/shard_map/pick_blocks/pallas_call | solution.py:90
  2.3 3.1 %collective-permute-start = (bf16[128,512]{1,0:T(8,128)(2,1)S(1)}, bf16[128,512]{1,0:T(8,128)(2,1)S(1)}, u32[]{:S(2)}, u32[]{:S(2)}) collective-permute-start(bf16[128,512]{1,0:T(8,128)(2,1)S(1)} %get-tuple-element.68), channel_id=1, source_target_pairs={{0,4},{1,9},{2,14},{3,11},{4,8},{5,13},{6,2},{7,15},{8,12},{9,1},{... | collective-permute-start | bytes 393224 | tf_op jit(solution)/shard_map/ppermute | solution.py:795
  5.4 1.6 %collective-permute-start.1 = (bf16[128,512]{1,0:T(8,128)(2,1)S(1)}, bf16[128,512]{1,0:T(8,128)(2,1)S(1)}, u32[]{:S(2)}, u32[]{:S(2)}) collective-permute-start(bf16[128,512]{1,0:T(8,128)(2,1)S(1)} %get-tuple-element.71), channel_id=1, source_target_pairs={{0,4},{1,9},{2,14},{3,11},{4,8},{5,13},{6,2},{7,15},{8,12},{9,1},{... | collective-permute-start | bytes 393224 | tf_op jit(solution)/shard_map/ppermute | solution.py:795
  7.0 2.0 %own_rows.1 = (bf16[512,512]{1,0:T(8,128)(2,1)S(1)}, bf16[1024,128]{1,0:T(8,128)(2,1)S(1)}, bf16[1024,128]{1,0:T(8,128)(2,1)S(1)}, bf16[512,128]{1,0:T(8,128)(2,...) custom-call(bf16[512,512]{1,0:T(8,128)(2,1)} %bitcast.12, ...), custom_call_target="tpu_custom_call" | custom-call | flops 1 | bytes 1 | tf_op jit(solution)/shard_map/own_rows/pallas_call | solution.py:183
  9.0 2.5 %collective-permute-done.refs_0_ = bf16[128,512]{1,0:T(8,128)(2,1)S(1)} collective-permute-done((bf16[128,512]{1,0:T(8,128)(2,1)S(1)}, bf16[128,512]{1,0:T(8,128)(2,1)S(1)}, u32[]{:S(2)}, u32[]{:S(2)}) %collective-permute-start) | collective-permute-done | bytes 131104 | tf_op jit(solution)/shard_map/ppermute | solution.py:795
  12.1 1.8 %collective-permute-done.1.refs_1_ = bf16[128,512]{1,0:T(8,128)(2,1)S(1)} collective-permute-done((bf16[128,512]{1,0:T(8,128)(2,1)S(1)}, bf16[128,512]{1,0:T(8,128)(2,1)S(1)}, u32[]{:S(2)}, u32[]{:S(2)}) %collective-permute-start.1) | collective-permute-done | bytes 131104 | tf_op jit(solution)/shard_map/ppermute | solution.py:795
  13.9 1.5 %collective-permute-start.3 = (bf16[64,512]{1,0:T(8,128)(2,1)S(1)}, bf16[64,512]{1,0:T(8,128)(2,1)S(1)}, u32[]{:S(2)}, u32[]{:S(2)}) collective-permute-start(bf16[64,512]{1,0:T(8,128)(2,1)S(1)} %get-tuple-element.132), channel_id=1, source_target_pairs={{0,1},{1,0},{2,3},{3,2},{4,5},{5,4},{6,7},{7,6},{8,9},{9,8},{10,11... | collective-permute-start | bytes 196616 | tf_op jit(solution)/shard_map/ppermute | solution.py:745
  18.1 3.3 %collective-permute-done.7.refs_6_ = bf16[128,512]{1,0:T(8,128)(2,1)S(1)} collective-permute-done((bf16[128,512]{1,0:T(8,128)(2,1)S(1)}, bf16[128,512]{1,0:T(8,128)(2,1)S(1)}, u32[]{:S(2)}, u32[]{:S(2)}) %collective-permute-start.7) | collective-permute-done | bytes 131104 | tf_op jit(solution)/shard_map/ppermute | solution.py:745
  21.9 0.8 %collective-permute-done.8.refs_7_ = bf16[128,512]{1,0:T(8,128)(2,1)S(1)} collective-permute-done((bf16[128,512]{1,0:T(8,128)(2,1)S(1)}, bf16[128,512]{1,0:T(8,128)(2,1)S(1)}, u32[]{:S(2)}, u32[]{:S(2)}) %collective-permute-start.8) | collective-permute-done | bytes 131104 | tf_op jit(solution)/shard_map/ppermute | solution.py:745
  22.9 5.1 %attention.1 = (bf16[1536,256]{1,0:T(8,128)(2,1)S(1)}, bf16[512,128]{1,0:T(8,128)(2,1)S(1)}, bf16[512,128]{1,0:T(8,128)(2,1)S(1)}, bf16[2,1088,128]{2,1,0:T(8,12...) custom-call(s32[4,3]{1,0:T(4,128)} %near_ref.1, ...), custom_call_target="tpu_custom_call" | custom-call | flops 1 | bytes 1 | tf_op jit(solution)/shard_map/attention/pallas_call | solution.py:400
  28.5 1.6 %collective-permute-start.11 = (bf16[128,512]{1,0:T(8,128)(2,1)S(1)}, bf16[128,512]{1,0:T(8,128)(2,1)S(1)}, u32[]{:S(2)}, u32[]{:S(2)}) collective-permute-start(bf16[128,512]{1,0:T(8,128)(2,1)S(1)} %get-tuple-element.98), channel_id=1, source_target_pairs={{0,16},{16,0},{1,17},{17,1},{2,18},{18,2},{3,19},{19,3},{4,20},{20... | collective-permute-start | bytes 393224 | tf_op jit(solution)/shard_map/ppermute | solution.py:745
  30.0 1.5 %collective-permute-start.13 = (bf16[128,512]{1,0:T(8,128)(2,1)S(1)}, bf16[128,512]{1,0:T(8,128)(2,1)S(1)}, u32[]{:S(2)}, u32[]{:S(2)}) collective-permute-start(bf16[128,512]{1,0:T(8,128)(2,1)S(1)} %get-tuple-element.103), channel_id=1, source_target_pairs={{0,4},{4,0},{8,12},{12,8},{1,5},{5,1},{9,13},{13,9},{2,6},{6,2},{1... | collective-permute-start | bytes 393224 | tf_op jit(solution)/shard_map/ppermute | solution.py:745
  31.5 0.9 %own_terms.1 = (bf16[2,1040,128]{2,1,0:T(8,128)(2,1)S(1)}, bf16[2,1040,128]{2,1,0:T(8,128)(2,1)S(1)}) custom-call(bf16[1536,256]{1,0:T(8,128)(2,1)S(1)} %get-tuple-element.90.both_ref, bf16[512,512]{1,0:T(8,128)(2,1)S(1)} %get-tuple-element.69.refs_9_.unit_ref, bf16[512,128]{1,0:T(8,128)(2,1)S(1)} %get-tuple-element.91.dq_ref, ...), custom_call_target="tpu_custom_call" | custom-call | flops 1 | bytes 1 | tf_op jit(solution)/shard_map/own_terms/pallas_call | solution.py:498
  32.6 2.7 %collective-permute-done.13.refs_3_ = bf16[128,512]{1,0:T(8,128)(2,1)S(1)} collective-permute-done((bf16[128,512]{1,0:T(8,128)(2,1)S(1)}, bf16[128,512]{1,0:T(8,128)(2,1)S(1)}, u32[]{:S(2)}, u32[]{:S(2)}) %collective-permute-start.13) | collective-permute-done | bytes 131104 | tf_op jit(solution)/shard_map/ppermute | solution.py:745
  35.4 1.6 %collective-permute-start.14 = (bf16[64,512]{1,0:T(8,128)(2,1)S(1)}, bf16[64,512]{1,0:T(8,128)(2,1)S(1)}, u32[]{:S(2)}, u32[]{:S(2)}) collective-permute-start(bf16[64,512]{1,0:T(8,128)(2,1)S(1)} %get-tuple-element.106), channel_id=1, source_target_pairs={{0,4},{4,0},{8,12},{12,8},{1,5},{5,1},{9,13},{13,9},{2,6},{6,2},{1... | collective-permute-start | bytes 196616 | tf_op jit(solution)/shard_map/ppermute | solution.py:745
  37.5 1.7 %collective-permute-start.17 = (bf16[1088,128]{1,0:T(8,128)(2,1)S(1)}, bf16[1088,128]{1,0:T(8,128)(2,1)S(1)}, u32[]{:S(2)}, u32[]{:S(2)}) collective-permute-start(bf16[1088,128]{1,0:T(8,128)(2,1)S(1)} %fusion), channel_id=1, source_target_pairs={{0,2},{1,3},{2,0},{3,1},{4,6},{5,7},{6,4},{7,5},{8,10},{9,11},{10,... | collective-permute-start | bytes 835592 | tf_op jit(solution)/shard_map/ppermute | solution.py:745
  39.7 1.5 %collective-permute-done.15.refs_3_ = bf16[64,512]{1,0:T(8,128)(2,1)S(1)} collective-permute-done((bf16[64,512]{1,0:T(8,128)(2,1)S(1)}, bf16[64,512]{1,0:T(8,128)(2,1)S(1)}, u32[]{:S(2)}, u32[]{:S(2)}) %collective-permute-start.15) | collective-permute-done | bytes 65568 | tf_op jit(solution)/shard_map/ppermute | solution.py:745
  41.4 1.8 %collective-permute-start.16 = (bf16[1040,128]{1,0:T(8,128)(2,1)S(1)}, bf16[1040,128]{1,0:T(8,128)(2,1)S(1)}, u32[]{:S(2)}, u32[]{:S(2)}) collective-permute-start(bf16[1040,128]{1,0:T(8,128)(2,1)S(1)} %fusion.1), channel_id=1, source_target_pairs={{0,2},{1,3},{2,0},{3,1},{4,6},{5,7},{6,4},{7,5},{8,10},{9,11},{10,... | collective-permute-start | bytes 798728 | tf_op jit(solution)/shard_map/ppermute | solution.py:745
  43.2 2.3 %collective-permute-start.21 = (bf16[128,512]{1,0:T(8,128)(2,1)S(1)}, bf16[128,512]{1,0:T(8,128)(2,1)S(1)}, u32[]{:S(2)}, u32[]{:S(2)}) collective-permute-start(bf16[128,512]{1,0:T(8,128)(2,1)S(1)} %total_grads.1.mine_ref), channel_id=1, source_target_pairs={{0,8},{4,12},{8,0},{12,4},{1,9},{5,13},{9,1},{13,5},{2,10},{6,14},... | collective-permute-start | bytes 393224 | tf_op jit(solution)/shard_map/ppermute | solution.py:745
  45.5 1.6 %collective-permute-done.17.last_ref = bf16[1088,128]{1,0:T(8,128)(2,1)S(1)} collective-permute-done((bf16[1088,128]{1,0:T(8,128)(2,1)S(1)}, bf16[1088,128]{1,0:T(8,128)(2,1)S(1)}, u32[]{:S(2)}, u32[]{:S(2)}) %collective-permute-start.17) | collective-permute-done | bytes 278560 | tf_op jit(solution)/shard_map/ppermute | solution.py:745
  47.2 2.5 %collective-permute-start.20 = (bf16[544,128]{1,0:T(8,128)(2,1)S(1)}, bf16[544,128]{1,0:T(8,128)(2,1)S(1)}, u32[]{:S(2)}, u32[]{:S(2)}) collective-permute-start(bf16[544,128]{1,0:T(8,128)(2,1)S(1)} %get-tuple-element.113), channel_id=1, source_target_pairs={{0,8},{4,12},{8,0},{12,4},{1,9},{5,13},{9,1},{13,5},{2,10},{6,14},... | collective-permute-start | bytes 417800 | tf_op jit(solution)/shard_map/ppermute | solution.py:750
  50.1 1.7 %collective-permute-start.19 = (bf16[272,128]{1,0:T(8,128)(2,1)S(1)}, bf16[272,128]{1,0:T(8,128)(2,1)S(1)}, u32[]{:S(2)}, u32[]{:S(2)}) collective-permute-start(bf16[272,128]{1,0:T(8,128)(2,1)S(1)} %get-tuple-element.112), channel_id=1, source_target_pairs={{0,4},{4,8},{8,12},{12,0},{1,5},{5,9},{9,13},{13,1},{2,6},{6,10},{... | collective-permute-start | bytes 208904 | tf_op jit(solution)/shard_map/ppermute | solution.py:750
  51.8 0.7 %own_sum.1 = (bf16[512,128]{1,0:T(8,128)(2,1)}, f32[528,128]{1,0:T(8,128)S(1)}) custom-call(bf16[2,1040,128]{2,1,0:T(8,128)(2,1)S(1)} %get-tuple-element.95.keep_ref, bf16[2,1040,128]{2,1,0:T(8,128)(2,1)S(1)} %collective-permute-done.10.got_ref, bf16[1040,128]{1,0:T(8,128)(2,1)S(1)} %collective-permute-done.16.last_ref), custom_call_target="tpu_custom_call" | custom-call | flops 1 | bytes 1 | tf_op jit(solution)/shard_map/own_sum/pallas_call | solution.py:644
  52.5 2.0 %collective-permute-done.21.got_ref = bf16[128,512]{1,0:T(8,128)(2,1)S(1)} collective-permute-done((bf16[128,512]{1,0:T(8,128)(2,1)S(1)}, bf16[128,512]{1,0:T(8,128)(2,1)S(1)}, u32[]{:S(2)}, u32[]{:S(2)}) %collective-permute-start.21) | collective-permute-done | bytes 131104 | tf_op jit(solution)/shard_map/ppermute | solution.py:745
  54.6 1.2 %collective-permute-start.23 = (bf16[64,512]{1,0:T(8,128)(2,1)S(1)}, bf16[64,512]{1,0:T(8,128)(2,1)S(1)}, u32[]{:S(2)}, u32[]{:S(2)}) collective-permute-start(bf16[64,512]{1,0:T(8,128)(2,1)S(1)} %get-tuple-element.122.refs_2_), channel_id=1, source_target_pairs={{0,16},{16,0},{1,17},{17,1},{2,18},{18,2},{3,19},{19,3},{4,20},{20... | collective-permute-start | bytes 196616 | tf_op jit(solution)/shard_map/ppermute | solution.py:745
  55.7 2.9 %collective-permute-done.18.refs_4_ = bf16[272,128]{1,0:T(8,128)(2,1)S(1)} collective-permute-done((bf16[272,128]{1,0:T(8,128)(2,1)S(1)}, bf16[272,128]{1,0:T(8,128)(2,1)S(1)}, u32[]{:S(2)}, u32[]{:S(2)}) %collective-permute-start.18) | collective-permute-done | bytes 69664 | tf_op jit(solution)/shard_map/ppermute | solution.py:750
  58.6 0.7 %collective-permute-done.22.refs_1_ = bf16[64,512]{1,0:T(8,128)(2,1)S(1)} collective-permute-done((bf16[64,512]{1,0:T(8,128)(2,1)S(1)}, bf16[64,512]{1,0:T(8,128)(2,1)S(1)}, u32[]{:S(2)}, u32[]{:S(2)}) %collective-permute-start.22) | collective-permute-done | bytes 65568 | tf_op jit(solution)/shard_map/ppermute | solution.py:745
  59.3 0.7 %collective-permute-start.24 = (bf16[128,512]{1,0:T(8,128)(2,1)S(1)}, bf16[128,512]{1,0:T(8,128)(2,1)S(1)}, u32[]{:S(2)}, u32[]{:S(2)}) collective-permute-start(bf16[128,512]{1,0:T(8,128)(2,1)S(1)} %get-tuple-element.123.refs_0_), channel_id=1, source_target_pairs={{0,16},{16,0},{1,17},{17,1},{2,18},{18,2},{3,19},{19,3},{4,20},{20... | collective-permute-start | bytes 393224 | tf_op jit(solution)/shard_map/ppermute | solution.py:745
  60.1 2.4 %collective-permute-start.25 = (bf16[128,512]{1,0:T(8,128)(2,1)S(1)}, bf16[128,512]{1,0:T(8,128)(2,1)S(1)}, u32[]{:S(2)}, u32[]{:S(2)}) collective-permute-start(bf16[128,512]{1,0:T(8,128)(2,1)S(1)} %get-tuple-element.125.refs_2_), channel_id=1, source_target_pairs={{0,4},{4,0},{8,12},{12,8},{1,5},{5,1},{9,13},{13,9},{2,6},{6,2},{1... | collective-permute-start | bytes 393224 | tf_op jit(solution)/shard_map/ppermute | solution.py:745
  62.5 1.5 %finish.1 = bf16[512,128]{1,0:T(8,128)(2,1)} custom-call(s32[2,4]{1,0:T(2,128)} %bitcast.16, f32[528,128]{1,0:T(8,128)S(1)} %get-tuple-element.116.refs_1_, f32[512,128]{1,0:T(8,128)S(1)} %get-tuple-element.117.refs_2_, f32[512,128]{1,0:T(8,128)S(1)} %get-tuple-element.118.refs_3_, bf16[272,128]{1,0:T(8,128)(2,1)S(1)} %collective-permute-done.18.refs_4_, ...), custom_call_target="tpu_custom_call" | custom-call | flops 1 | bytes 1 | tf_op jit(solution)/shard_map/finish/pallas_call | solution.py:696
  64.4 1.1 %collective-permute-done.25.refs_3_ = bf16[128,512]{1,0:T(8,128)(2,1)S(1)} collective-permute-done((bf16[128,512]{1,0:T(8,128)(2,1)S(1)}, bf16[128,512]{1,0:T(8,128)(2,1)S(1)}, u32[]{:S(2)}, u32[]{:S(2)}) %collective-permute-start.25) | collective-permute-done | bytes 131104 | tf_op jit(solution)/shard_map/ppermute | solution.py:745
  65.5 1.2 %weight_grads.1 = (f32[512,128]{1,0:T(8,128)}, f32[512,128]{1,0:T(8,128)}, f32[512,128]{1,0:T(8,128)}, f32[128,512]{1,0:T(8,128)}) custom-call(bf16[128,512]{1,0:T(8,128)(2,1)S(1)} %get-tuple-element.123.refs_0_, bf16[128,512]{1,0:T(8,128)(2,1)S(1)} %collective-permute-done.24.refs_1_, bf16[128,512]{1,0:T(8,128)(2,1)S(1)} %get-tuple-element.125.refs_2_, ...), custom_call_target="tpu_custom_call" | custom-call | flops 1 | bytes 1 | tf_op jit(solution)/shard_map/weight_grads/pallas_call | solution.py:733
  (37 shorter events, 6.5 us)
Async XLA Ops:
  2.3 9.2 %collective-permute-start = (bf16[128,512]{1,0:T(8,128)(2,1)S(1)}, bf16[128,512]{1,0:T(8,128)(2,1)S(1)}, u32[]{:S(2)}, u32[]{:S(2)}) collective-permute-start(bf16[128,512]{1,0:T(8,128)(2,1)S(1)} %get-tuple-element.68), channel_id=1, source_target_pairs={{0,4},{1,9},{2,14},{3,11},{4,8},{5,13},{6,2},{7,15},{8,12},{9,1},{... | collective-permute-start | bytes 393224 | tf_op jit(solution)/shard_map/ppermute | solution.py:795
  5.4 8.5 %collective-permute-start.1 = (bf16[128,512]{1,0:T(8,128)(2,1)S(1)}, bf16[128,512]{1,0:T(8,128)(2,1)S(1)}, u32[]{:S(2)}, u32[]{:S(2)}) collective-permute-start(bf16[128,512]{1,0:T(8,128)(2,1)S(1)} %get-tuple-element.71), channel_id=1, source_target_pairs={{0,4},{1,9},{2,14},{3,11},{4,8},{5,13},{6,2},{7,15},{8,12},{9,1},{... | collective-permute-start | bytes 393224 | tf_op jit(solution)/shard_map/ppermute | solution.py:795
  11.6 9.8 %collective-permute-start.6 = (bf16[128,512]{1,0:T(8,128)(2,1)S(1)}, bf16[128,512]{1,0:T(8,128)(2,1)S(1)}, u32[]{:S(2)}, u32[]{:S(2)}) collective-permute-start(bf16[128,512]{1,0:T(8,128)(2,1)S(1)} %collective-permute-done.refs_0_), channel_id=1, source_target_pairs={{0,2},{1,3},{2,0},{3,1},{4,6},{5,7},{6,4},{7,5},{8,10},{9,11},{10,... | collective-permute-start | bytes 393224 | tf_op jit(solution)/shard_map/ppermute | solution.py:745
  13.9 2.4 %collective-permute-start.3 = (bf16[64,512]{1,0:T(8,128)(2,1)S(1)}, bf16[64,512]{1,0:T(8,128)(2,1)S(1)}, u32[]{:S(2)}, u32[]{:S(2)}) collective-permute-start(bf16[64,512]{1,0:T(8,128)(2,1)S(1)} %get-tuple-element.132), channel_id=1, source_target_pairs={{0,1},{1,0},{2,3},{3,2},{4,5},{5,4},{6,7},{7,6},{8,9},{9,8},{10,11... | collective-permute-start | bytes 196616 | tf_op jit(solution)/shard_map/ppermute | solution.py:745
  15.5 1.3 %collective-permute-start.2 = (bf16[64,512]{1,0:T(8,128)(2,1)S(1)}, bf16[64,512]{1,0:T(8,128)(2,1)S(1)}, u32[]{:S(2)}, u32[]{:S(2)}) collective-permute-start(bf16[64,512]{1,0:T(8,128)(2,1)S(1)} %get-tuple-element.133), channel_id=1, source_target_pairs={{0,1},{1,0},{2,3},{3,2},{4,5},{5,4},{6,7},{7,6},{8,9},{9,8},{10,11... | collective-permute-start | bytes 196616 | tf_op jit(solution)/shard_map/ppermute | solution.py:745
  15.5 5.8 %collective-permute-start.7 = (bf16[128,512]{1,0:T(8,128)(2,1)S(1)}, bf16[128,512]{1,0:T(8,128)(2,1)S(1)}, u32[]{:S(2)}, u32[]{:S(2)}) collective-permute-start(bf16[128,512]{1,0:T(8,128)(2,1)S(1)} %collective-permute-done.1.refs_1_), channel_id=1, source_target_pairs={{0,2},{1,3},{2,0},{3,1},{4,6},{5,7},{6,4},{7,5},{8,10},{9,11},{10,... | collective-permute-start | bytes 393224 | tf_op jit(solution)/shard_map/ppermute | solution.py:745
  15.9 1.3 %collective-permute-start.5 = (bf16[64,512]{1,0:T(8,128)(2,1)S(1)}, bf16[64,512]{1,0:T(8,128)(2,1)S(1)}, u32[]{:S(2)}, u32[]{:S(2)}) collective-permute-start(bf16[64,512]{1,0:T(8,128)(2,1)S(1)} %get-tuple-element.130), channel_id=1, source_target_pairs={{0,1},{1,0},{2,3},{3,2},{4,5},{5,4},{6,7},{7,6},{8,9},{9,8},{10,11... | collective-permute-start | bytes 196616 | tf_op jit(solution)/shard_map/ppermute | solution.py:745
  16.4 1.3 %collective-permute-start.4 = (bf16[64,512]{1,0:T(8,128)(2,1)S(1)}, bf16[64,512]{1,0:T(8,128)(2,1)S(1)}, u32[]{:S(2)}, u32[]{:S(2)}) collective-permute-start(bf16[64,512]{1,0:T(8,128)(2,1)S(1)} %get-tuple-element.131), channel_id=1, source_target_pairs={{0,1},{1,0},{2,3},{3,2},{4,5},{5,4},{6,7},{7,6},{8,9},{9,8},{10,11... | collective-permute-start | bytes 196616 | tf_op jit(solution)/shard_map/ppermute | solution.py:745
  21.4 1.3 %collective-permute-start.8 = (bf16[128,512]{1,0:T(8,128)(2,1)S(1)}, bf16[128,512]{1,0:T(8,128)(2,1)S(1)}, u32[]{:S(2)}, u32[]{:S(2)}) collective-permute-start(bf16[128,512]{1,0:T(8,128)(2,1)S(1)} %collective-permute-done.6.refs_5_), channel_id=1, source_target_pairs={{0,1},{1,0},{2,3},{3,2},{4,5},{5,4},{6,7},{7,6},{8,9},{9,8},{10,11... | collective-permute-start | bytes 393224 | tf_op jit(solution)/shard_map/ppermute | solution.py:745
  21.4 1.5 %collective-permute-start.9 = (bf16[128,512]{1,0:T(8,128)(2,1)S(1)}, bf16[128,512]{1,0:T(8,128)(2,1)S(1)}, u32[]{:S(2)}, u32[]{:S(2)}) collective-permute-start(bf16[128,512]{1,0:T(8,128)(2,1)S(1)} %collective-permute-done.7.refs_6_), channel_id=1, source_target_pairs={{0,1},{1,0},{2,3},{3,2},{4,5},{5,4},{6,7},{7,6},{8,9},{9,8},{10,11... | collective-permute-start | bytes 393224 | tf_op jit(solution)/shard_map/ppermute | solution.py:745
  28.1 4.5 %collective-permute-start.12 = (bf16[2,1088,128]{2,1,0:T(8,128)(2,1)S(1)}, bf16[2,1088,128]{2,1,0:T(8,128)(2,1)S(1)}, u32[]{:S(2)}, u32[]{:S(2)}) collective-permute-start(bf16[2,1088,128]{2,1,0:T(8,128)(2,1)S(1)} %get-tuple-element.100), channel_id=1, source_target_pairs={{0,1},{1,0},{2,3},{3,2},{4,5},{5,4},{6,7},{7,6},{8,9},{9,8},{10,11... | collective-permute-start | bytes 1671176 | tf_op jit(solution)/shard_map/ppermute | solution.py:745
  28.5 6.9 %collective-permute-start.11 = (bf16[128,512]{1,0:T(8,128)(2,1)S(1)}, bf16[128,512]{1,0:T(8,128)(2,1)S(1)}, u32[]{:S(2)}, u32[]{:S(2)}) collective-permute-start(bf16[128,512]{1,0:T(8,128)(2,1)S(1)} %get-tuple-element.98), channel_id=1, source_target_pairs={{0,16},{16,0},{1,17},{17,1},{2,18},{18,2},{3,19},{19,3},{4,20},{20... | collective-permute-start | bytes 393224 | tf_op jit(solution)/shard_map/ppermute | solution.py:745
  30.0 5.3 %collective-permute-start.13 = (bf16[128,512]{1,0:T(8,128)(2,1)S(1)}, bf16[128,512]{1,0:T(8,128)(2,1)S(1)}, u32[]{:S(2)}, u32[]{:S(2)}) collective-permute-start(bf16[128,512]{1,0:T(8,128)(2,1)S(1)} %get-tuple-element.103), channel_id=1, source_target_pairs={{0,4},{4,0},{8,12},{12,8},{1,5},{5,1},{9,13},{13,9},{2,6},{6,2},{1... | collective-permute-start | bytes 393224 | tf_op jit(solution)/shard_map/ppermute | solution.py:745
  32.4 8.8 %collective-permute-start.10 = (bf16[2,1040,128]{2,1,0:T(8,128)(2,1)S(1)}, bf16[2,1040,128]{2,1,0:T(8,128)(2,1)S(1)}, u32[]{:S(2)}, u32[]{:S(2)}) collective-permute-start(bf16[2,1040,128]{2,1,0:T(8,128)(2,1)S(1)} %get-tuple-element.96), channel_id=1, source_target_pairs={{0,1},{1,0},{2,3},{3,2},{4,5},{5,4},{6,7},{7,6},{8,9},{9,8},{10,11... | collective-permute-start | bytes 1597448 | tf_op jit(solution)/shard_map/ppermute | solution.py:745
  35.4 4.3 %collective-permute-start.14 = (bf16[64,512]{1,0:T(8,128)(2,1)S(1)}, bf16[64,512]{1,0:T(8,128)(2,1)S(1)}, u32[]{:S(2)}, u32[]{:S(2)}) collective-permute-start(bf16[64,512]{1,0:T(8,128)(2,1)S(1)} %get-tuple-element.106), channel_id=1, source_target_pairs={{0,4},{4,0},{8,12},{12,8},{1,5},{5,1},{9,13},{13,9},{2,6},{6,2},{1... | collective-permute-start | bytes 196616 | tf_op jit(solution)/shard_map/ppermute | solution.py:745
  37.0 4.3 %collective-permute-start.15 = (bf16[64,512]{1,0:T(8,128)(2,1)S(1)}, bf16[64,512]{1,0:T(8,128)(2,1)S(1)}, u32[]{:S(2)}, u32[]{:S(2)}) collective-permute-start(bf16[64,512]{1,0:T(8,128)(2,1)S(1)} %get-tuple-element.108), channel_id=1, source_target_pairs={{0,16},{16,0},{1,17},{17,1},{2,18},{18,2},{3,19},{19,3},{4,20},{20... | collective-permute-start | bytes 196616 | tf_op jit(solution)/shard_map/ppermute | solution.py:745
  37.5 9.6 %collective-permute-start.17 = (bf16[1088,128]{1,0:T(8,128)(2,1)S(1)}, bf16[1088,128]{1,0:T(8,128)(2,1)S(1)}, u32[]{:S(2)}, u32[]{:S(2)}) collective-permute-start(bf16[1088,128]{1,0:T(8,128)(2,1)S(1)} %fusion), channel_id=1, source_target_pairs={{0,2},{1,3},{2,0},{3,1},{4,6},{5,7},{6,4},{7,5},{8,10},{9,11},{10,... | collective-permute-start | bytes 835592 | tf_op jit(solution)/shard_map/ppermute | solution.py:745
  41.4 10.4 %collective-permute-start.16 = (bf16[1040,128]{1,0:T(8,128)(2,1)S(1)}, bf16[1040,128]{1,0:T(8,128)(2,1)S(1)}, u32[]{:S(2)}, u32[]{:S(2)}) collective-permute-start(bf16[1040,128]{1,0:T(8,128)(2,1)S(1)} %fusion.1), channel_id=1, source_target_pairs={{0,2},{1,3},{2,0},{3,1},{4,6},{5,7},{6,4},{7,5},{8,10},{9,11},{10,... | collective-permute-start | bytes 798728 | tf_op jit(solution)/shard_map/ppermute | solution.py:745
  43.2 11.2 %collective-permute-start.21 = (bf16[128,512]{1,0:T(8,128)(2,1)S(1)}, bf16[128,512]{1,0:T(8,128)(2,1)S(1)}, u32[]{:S(2)}, u32[]{:S(2)}) collective-permute-start(bf16[128,512]{1,0:T(8,128)(2,1)S(1)} %total_grads.1.mine_ref), channel_id=1, source_target_pairs={{0,8},{4,12},{8,0},{12,4},{1,9},{5,13},{9,1},{13,5},{2,10},{6,14},... | collective-permute-start | bytes 393224 | tf_op jit(solution)/shard_map/ppermute | solution.py:745
  47.2 12.1 %collective-permute-start.20 = (bf16[544,128]{1,0:T(8,128)(2,1)S(1)}, bf16[544,128]{1,0:T(8,128)(2,1)S(1)}, u32[]{:S(2)}, u32[]{:S(2)}) collective-permute-start(bf16[544,128]{1,0:T(8,128)(2,1)S(1)} %get-tuple-element.113), channel_id=1, source_target_pairs={{0,8},{4,12},{8,0},{12,4},{1,9},{5,13},{9,1},{13,5},{2,10},{6,14},... | collective-permute-start | bytes 417800 | tf_op jit(solution)/shard_map/ppermute | solution.py:750
  49.7 8.8 %collective-permute-start.18 = (bf16[272,128]{1,0:T(8,128)(2,1)S(1)}, bf16[272,128]{1,0:T(8,128)(2,1)S(1)}, u32[]{:S(2)}, u32[]{:S(2)}) collective-permute-start(bf16[272,128]{1,0:T(8,128)(2,1)S(1)} %get-tuple-element.111), channel_id=1, source_target_pairs={{0,12},{4,0},{8,4},{12,8},{1,13},{5,1},{9,5},{13,9},{2,14},{6,2},{... | collective-permute-start | bytes 208904 | tf_op jit(solution)/shard_map/ppermute | solution.py:750
  50.1 8.5 %collective-permute-start.19 = (bf16[272,128]{1,0:T(8,128)(2,1)S(1)}, bf16[272,128]{1,0:T(8,128)(2,1)S(1)}, u32[]{:S(2)}, u32[]{:S(2)}) collective-permute-start(bf16[272,128]{1,0:T(8,128)(2,1)S(1)} %get-tuple-element.112), channel_id=1, source_target_pairs={{0,4},{4,8},{8,12},{12,0},{1,5},{5,9},{9,13},{13,1},{2,6},{6,10},{... | collective-permute-start | bytes 208904 | tf_op jit(solution)/shard_map/ppermute | solution.py:750
  54.5 4.8 %collective-permute-start.22 = (bf16[64,512]{1,0:T(8,128)(2,1)S(1)}, bf16[64,512]{1,0:T(8,128)(2,1)S(1)}, u32[]{:S(2)}, u32[]{:S(2)}) collective-permute-start(bf16[64,512]{1,0:T(8,128)(2,1)S(1)} %get-tuple-element.120.refs_0_), channel_id=1, source_target_pairs={{0,4},{4,0},{8,12},{12,8},{1,5},{5,1},{9,13},{13,9},{2,6},{6,2},{1... | collective-permute-start | bytes 196616 | tf_op jit(solution)/shard_map/ppermute | solution.py:745
  54.6 4.8 %collective-permute-start.23 = (bf16[64,512]{1,0:T(8,128)(2,1)S(1)}, bf16[64,512]{1,0:T(8,128)(2,1)S(1)}, u32[]{:S(2)}, u32[]{:S(2)}) collective-permute-start(bf16[64,512]{1,0:T(8,128)(2,1)S(1)} %get-tuple-element.122.refs_2_), channel_id=1, source_target_pairs={{0,16},{16,0},{1,17},{17,1},{2,18},{18,2},{3,19},{19,3},{4,20},{20... | collective-permute-start | bytes 196616 | tf_op jit(solution)/shard_map/ppermute | solution.py:745
  59.3 5.0 %collective-permute-start.24 = (bf16[128,512]{1,0:T(8,128)(2,1)S(1)}, bf16[128,512]{1,0:T(8,128)(2,1)S(1)}, u32[]{:S(2)}, u32[]{:S(2)}) collective-permute-start(bf16[128,512]{1,0:T(8,128)(2,1)S(1)} %get-tuple-element.123.refs_0_), channel_id=1, source_target_pairs={{0,16},{16,0},{1,17},{17,1},{2,18},{18,2},{3,19},{19,3},{4,20},{20... | collective-permute-start | bytes 393224 | tf_op jit(solution)/shard_map/ppermute | solution.py:745
  60.1 5.4 %collective-permute-start.25 = (bf16[128,512]{1,0:T(8,128)(2,1)S(1)}, bf16[128,512]{1,0:T(8,128)(2,1)S(1)}, u32[]{:S(2)}, u32[]{:S(2)}) collective-permute-start(bf16[128,512]{1,0:T(8,128)(2,1)S(1)} %get-tuple-element.125.refs_2_), channel_id=1, source_target_pairs={{0,4},{4,0},{8,12},{12,8},{1,5},{5,1},{9,13},{13,9},{2,6},{6,2},{1... | collective-permute-start | bytes 393224 | tf_op jit(solution)/shard_map/ppermute | solution.py:745
where the time goes:
time: 66.9 us; the launch traced here: 66.7 us
  starting transfers between devices  28.8 us (43%)
  waiting for transfers between devices  23.1 us (35%)
  Pallas kernels  13.9 us (21%)
  between operations  0.77 us (1%)
    ppermute x21, starting transfers between devices, swap(): lax.ppermute(array, axis, [(i, i ^ bit) for i in range(lax.axis_size(axis...  19.5 us
    ppermute x21, waiting for transfers between devices, swap(): lax.ppermute(array, axis, [(i, i ^ bit) for i in range(lax.axis_size(axis...  15.9 us
    pallas_call x1, Pallas kernels, run_attend(): pl.pallas_call(functools.partial(attend_kernel, cfg), out_shape=[shape((e...  5.14 us
    ppermute x2, starting transfers between devices, body(): lax.ppermute(block, ('dom', 'tensor'), route)  4.65 us
    ppermute x3, starting transfers between devices, shifted(): lax.ppermute(array, axis, [(i, (i + distance) % size) for i in range(size)])  4.57 us
    ppermute x2, waiting for transfers between devices, body(): lax.ppermute(block, ('dom', 'tensor'), route)  4.29 us
    ppermute x3, waiting for transfers between devices, shifted(): lax.ppermute(array, axis, [(i, (i + distance) % size) for i in range(size)])  2.88 us
    pallas_call x1, Pallas kernels, run_own(): pl.pallas_call(own_kernel, out_shape=(shape((rows, feats), BF16), shape((...  2.04 us
  transfers between devices with their start and end apart: 26, of which 17 were waited for; matrix products, arithmetic and copies ran while one was open for 0% of the time, Pallas kernels for 9%

commit v1 on v0

--- a/solution.py
+++ b/solution.py
@@ -67,21 +67,19 @@
 
 
 def pick_kernel(ranks, share, send_ref, states_ref, *refs):
-    outs, table, sems = refs[:share], refs[share], refs[share + 1]
+    outs, (table, held, sems) = refs[:share], refs[share:]
     rank = lax.axis_index("tensor")
-    fetch = pltpu.make_async_copy(send_ref, table, sems.at[share])
-    fetch.start()
-    fetch.wait()
-    copies = []
+    copies = [
+        pltpu.make_async_copy(send_ref, table, sems.at[0]),
+        pltpu.make_async_copy(states_ref, held, sems.at[1]),
+    ]
+    for copy in copies:
+        copy.start()
+    for copy in copies:
+        copy.wait()
     for inner, out_ref in enumerate(outs):
         piece = rank_piece(rank, ranks, share, inner)
-        block = table[piece % SEND, piece // SEND]
-        copies.append(
-            pltpu.make_async_copy(states_ref.at[block_at(block), :], out_ref, sems.at[inner])
-        )
-        copies[-1].start()
-    for copy in copies:
-        copy.wait()
+        out_ref[...] = held[block_at(table[piece % SEND, piece // SEND]), :]
 
 
 def pick_blocks(states, send, ranks, share):
@@ -94,7 +92,8 @@
         out_specs=[vmem] * share,
         scratch_shapes=[
             pltpu.SMEM(send.shape, jnp.int32),
-            pltpu.SemaphoreType.DMA((share + 1,)),
+            pltpu.VMEM(states.shape, BF16),
+            pltpu.SemaphoreType.DMA((2,)),
         ],
         compiler_params=pltpu.CompilerParams(vmem_limit_bytes=SMALL),
         cost_estimate=BRIEF,
@@ -710,31 +709,52 @@
 
 
 def grads_kernel(factor, *refs):
-    first_held, first_got, second_held, second_got, q_ref, k_ref, v_ref, o_ref = refs
+    first_held, first_got, second_held, second_got = refs[:4]
+    results, made, sems = refs[4:8], refs[8:12], refs[12]
     dp, low, _ = my_bits()
     first, second = jnp.equal(dp, 1), jnp.equal(low, 1)
+    copies = [
+        pltpu.make_async_copy(source, target, sems.at[index])
+        for index, (source, target) in enumerate(zip(made, results))
+    ]
 
     def picked(flag, left, right, start):
         columns = slice(start, start + BLK)
         return jnp.where(flag, left[:, columns].astype(F32), right[:, columns].astype(F32)) * factor
 
-    for start in range(0, q_ref.shape[0], BLK):
-        rows = slice(start, start + BLK)
-        q_ref[rows, :] = picked(first, first_got, first_held, start).T
-        k_ref[rows, :] = picked(first, first_held, first_got, start).T
-        v_ref[rows, :] = picked(second, second_got, second_held, start).T
-        o_ref[:, rows] = picked(second, second_held, second_got, start)
+    picks = (
+        (first, first_got, first_held),
+        (first, first_held, first_got),
+        (second, second_got, second_held),
+        (second, second_held, second_got),
+    )
+    for index in (3, 0, 1, 2):
+        for start in range(0, first_held.shape[1], BLK):
+            rows = slice(start, start + BLK)
+            block = picked(*picks[index], start)
+            if index == 3:
+                made[index][:, rows] = block
+            else:
+                made[index][rows, :] = block.T
+        copies[index].start()
+    for copy in copies:
+        copy.wait()
 
 
 def run_grads(factor, *arrays):
     width, feats = arrays[0].shape
     vmem = pl.BlockSpec(memory_space=pltpu.VMEM)
-    tall = jax.ShapeDtypeStruct((feats, width), F32)
+    hbm = pl.BlockSpec(memory_space=pltpu.HBM)
+    shapes = [(feats, width)] * 3 + [(width, feats)]
     return pl.pallas_call(
         functools.partial(grads_kernel, factor),
-        out_shape=(tall, tall, tall, jax.ShapeDtypeStruct((width, feats), F32)),
+        out_shape=[jax.ShapeDtypeStruct(shape, F32) for shape in shapes],
         in_specs=[vmem] * 4,
-        out_specs=[vmem] * 4,
+        out_specs=[hbm] * 4,
+        scratch_shapes=[
+            *[pltpu.VMEM(shape, F32) for shape in shapes],
+            pltpu.SemaphoreType.DMA((4,)),
+        ],
         compiler_params=pltpu.CompilerParams(vmem_limit_bytes=SMALL),
         cost_estimate=BRIEF,
         name="weight_grads",

time: 66.9 us -> 66.3 us (level)
  no operation moved by 1% of the time
where the time goes in v1:
time: 66.3 us; the launch traced here: 66.1 us
  starting transfers between devices  28.8 us (43%)
  waiting for transfers between devices  23 us (35%)
  Pallas kernels  13.3 us (20%)
  between operations  0.77 us (1%)
    ppermute x21, starting transfers between devices, swap(): lax.ppermute(array, axis, [(i, i ^ bit) for i in range(lax.axis_size(axis...  19.6 us
    ppermute x21, waiting for transfers between devices, swap(): lax.ppermute(array, axis, [(i, i ^ bit) for i in range(lax.axis_size(axis...  15.9 us
    pallas_call x1, Pallas kernels, run_attend(): pl.pallas_call(functools.partial(attend_kernel, cfg), out_shape=[shape((e...  5.14 us
    ppermute x2, starting transfers between devices, body(): lax.ppermute(block, ('dom', 'tensor'), route)  4.65 us
    ppermute x3, starting transfers between devices, shifted(): lax.ppermute(array, axis, [(i, (i + distance) % size) for i in range(size)])  4.57 us
    ppermute x2, waiting for transfers between devices, body(): lax.ppermute(block, ('dom', 'tensor'), route)  4.3 us
    ppermute x3, waiting for transfers between devices, shifted(): lax.ppermute(array, axis, [(i, (i + distance) % size) for i in range(size)])  2.85 us
    pallas_call x1, Pallas kernels, run_own(): pl.pallas_call(own_kernel, out_shape=(shape((rows, feats), BF16), shape((...  2.04 us
  transfers between devices with their start and end apart: 26, of which 17 were waited for; matrix products, arithmetic and copies ran while one was open for 0% of the time, Pallas kernels for 9%

profile of v1, /device:TPU:0, one launch (start us, length us, event | category | flops | bytes accessed | tf_op | source)
XLA Modules:
  0.0 66.1 jit_solution(15612148317257147408)
XLA Ops:
  0.6 1.1 %pick_blocks.1 = (bf16[128,512]{1,0:T(8,128)(2,1)S(1)}, bf16[128,512]{1,0:T(8,128)(2,1)S(1)}) custom-call(s32[2,4]{1,0:T(2,128)} %bitcast.15, bf16[512,512]{1,0:T(8,128)(2,1)} %bitcast.11), custom_call_target="tpu_custom_call" | custom-call | flops 1 | bytes 1 | tf_op jit(solution)/shard_map/pick_blocks/pallas_call | solution.py:88
  1.7 3.1 %collective-permute-start = (bf16[128,512]{1,0:T(8,128)(2,1)S(1)}, bf16[128,512]{1,0:T(8,128)(2,1)S(1)}, u32[]{:S(2)}, u32[]{:S(2)}) collective-permute-start(bf16[128,512]{1,0:T(8,128)(2,1)S(1)} %get-tuple-element.68), channel_id=1, source_target_pairs={{0,4},{1,9},{2,14},{3,11},{4,8},{5,13},{6,2},{7,15},{8,12},{9,1},{... | collective-permute-start | bytes 393224 | tf_op jit(solution)/shard_map/ppermute | solution.py:815
  4.8 1.6 %collective-permute-start.1 = (bf16[128,512]{1,0:T(8,128)(2,1)S(1)}, bf16[128,512]{1,0:T(8,128)(2,1)S(1)}, u32[]{:S(2)}, u32[]{:S(2)}) collective-permute-start(bf16[128,512]{1,0:T(8,128)(2,1)S(1)} %get-tuple-element.71), channel_id=1, source_target_pairs={{0,4},{1,9},{2,14},{3,11},{4,8},{5,13},{6,2},{7,15},{8,12},{9,1},{... | collective-permute-start | bytes 393224 | tf_op jit(solution)/shard_map/ppermute | solution.py:815
  6.4 2.0 %own_rows.1 = (bf16[512,512]{1,0:T(8,128)(2,1)S(1)}, bf16[1024,128]{1,0:T(8,128)(2,1)S(1)}, bf16[1024,128]{1,0:T(8,128)(2,1)S(1)}, bf16[512,128]{1,0:T(8,128)(2,...) custom-call(bf16[512,512]{1,0:T(8,128)(2,1)} %bitcast.12, ...), custom_call_target="tpu_custom_call" | custom-call | flops 1 | bytes 1 | tf_op jit(solution)/shard_map/own_rows/pallas_call | solution.py:182
  8.4 2.5 %collective-permute-done.refs_0_ = bf16[128,512]{1,0:T(8,128)(2,1)S(1)} collective-permute-done((bf16[128,512]{1,0:T(8,128)(2,1)S(1)}, bf16[128,512]{1,0:T(8,128)(2,1)S(1)}, u32[]{:S(2)}, u32[]{:S(2)}) %collective-permute-start) | collective-permute-done | bytes 131104 | tf_op jit(solution)/shard_map/ppermute | solution.py:815
  11.5 1.8 %collective-permute-done.1.refs_1_ = bf16[128,512]{1,0:T(8,128)(2,1)S(1)} collective-permute-done((bf16[128,512]{1,0:T(8,128)(2,1)S(1)}, bf16[128,512]{1,0:T(8,128)(2,1)S(1)}, u32[]{:S(2)}, u32[]{:S(2)}) %collective-permute-start.1) | collective-permute-done | bytes 131104 | tf_op jit(solution)/shard_map/ppermute | solution.py:815
  13.3 1.5 %collective-permute-start.3 = (bf16[64,512]{1,0:T(8,128)(2,1)S(1)}, bf16[64,512]{1,0:T(8,128)(2,1)S(1)}, u32[]{:S(2)}, u32[]{:S(2)}) collective-permute-start(bf16[64,512]{1,0:T(8,128)(2,1)S(1)} %get-tuple-element.132), channel_id=1, source_target_pairs={{0,1},{1,0},{2,3},{3,2},{4,5},{5,4},{6,7},{7,6},{8,9},{9,8},{10,11... | collective-permute-start | bytes 196616 | tf_op jit(solution)/shard_map/ppermute | solution.py:765
  17.4 3.3 %collective-permute-done.7.refs_6_ = bf16[128,512]{1,0:T(8,128)(2,1)S(1)} collective-permute-done((bf16[128,512]{1,0:T(8,128)(2,1)S(1)}, bf16[128,512]{1,0:T(8,128)(2,1)S(1)}, u32[]{:S(2)}, u32[]{:S(2)}) %collective-permute-start.7) | collective-permute-done | bytes 131104 | tf_op jit(solution)/shard_map/ppermute | solution.py:765
  21.3 0.8 %collective-permute-done.8.refs_7_ = bf16[128,512]{1,0:T(8,128)(2,1)S(1)} collective-permute-done((bf16[128,512]{1,0:T(8,128)(2,1)S(1)}, bf16[128,512]{1,0:T(8,128)(2,1)S(1)}, u32[]{:S(2)}, u32[]{:S(2)}) %collective-permute-start.8) | collective-permute-done | bytes 131104 | tf_op jit(solution)/shard_map/ppermute | solution.py:765
  22.3 5.1 %attention.1 = (bf16[1536,256]{1,0:T(8,128)(2,1)S(1)}, bf16[512,128]{1,0:T(8,128)(2,1)S(1)}, bf16[512,128]{1,0:T(8,128)(2,1)S(1)}, bf16[2,1088,128]{2,1,0:T(8,12...) custom-call(s32[4,3]{1,0:T(4,128)} %near_ref.1, ...), custom_call_target="tpu_custom_call" | custom-call | flops 1 | bytes 1 | tf_op jit(solution)/shard_map/attention/pallas_call | solution.py:399
  27.8 1.6 %collective-permute-start.11 = (bf16[128,512]{1,0:T(8,128)(2,1)S(1)}, bf16[128,512]{1,0:T(8,128)(2,1)S(1)}, u32[]{:S(2)}, u32[]{:S(2)}) collective-permute-start(bf16[128,512]{1,0:T(8,128)(2,1)S(1)} %get-tuple-element.98), channel_id=1, source_target_pairs={{0,16},{16,0},{1,17},{17,1},{2,18},{18,2},{3,19},{19,3},{4,20},{20... | collective-permute-start | bytes 393224 | tf_op jit(solution)/shard_map/ppermute | solution.py:765
  29.4 1.5 %collective-permute-start.13 = (bf16[128,512]{1,0:T(8,128)(2,1)S(1)}, bf16[128,512]{1,0:T(8,128)(2,1)S(1)}, u32[]{:S(2)}, u32[]{:S(2)}) collective-permute-start(bf16[128,512]{1,0:T(8,128)(2,1)S(1)} %get-tuple-element.103), channel_id=1, source_target_pairs={{0,4},{4,0},{8,12},{12,8},{1,5},{5,1},{9,13},{13,9},{2,6},{6,2},{1... | collective-permute-start | bytes 393224 | tf_op jit(solution)/shard_map/ppermute | solution.py:765
  30.9 0.9 %own_terms.1 = (bf16[2,1040,128]{2,1,0:T(8,128)(2,1)S(1)}, bf16[2,1040,128]{2,1,0:T(8,128)(2,1)S(1)}) custom-call(bf16[1536,256]{1,0:T(8,128)(2,1)S(1)} %get-tuple-element.90.both_ref, bf16[512,512]{1,0:T(8,128)(2,1)S(1)} %get-tuple-element.69.refs_9_.unit_ref, bf16[512,128]{1,0:T(8,128)(2,1)S(1)} %get-tuple-element.91.dq_ref, ...), custom_call_target="tpu_custom_call" | custom-call | flops 1 | bytes 1 | tf_op jit(solution)/shard_map/own_terms/pallas_call | solution.py:497
  32.0 2.7 %collective-permute-done.13.refs_3_ = bf16[128,512]{1,0:T(8,128)(2,1)S(1)} collective-permute-done((bf16[128,512]{1,0:T(8,128)(2,1)S(1)}, bf16[128,512]{1,0:T(8,128)(2,1)S(1)}, u32[]{:S(2)}, u32[]{:S(2)}) %collective-permute-start.13) | collective-permute-done | bytes 131104 | tf_op jit(solution)/shard_map/ppermute | solution.py:765
  34.8 1.6 %collective-permute-start.14 = (bf16[64,512]{1,0:T(8,128)(2,1)S(1)}, bf16[64,512]{1,0:T(8,128)(2,1)S(1)}, u32[]{:S(2)}, u32[]{:S(2)}) collective-permute-start(bf16[64,512]{1,0:T(8,128)(2,1)S(1)} %get-tuple-element.106), channel_id=1, source_target_pairs={{0,4},{4,0},{8,12},{12,8},{1,5},{5,1},{9,13},{13,9},{2,6},{6,2},{1... | collective-permute-start | bytes 196616 | tf_op jit(solution)/shard_map/ppermute | solution.py:765
  36.9 1.8 %collective-permute-start.17 = (bf16[1088,128]{1,0:T(8,128)(2,1)S(1)}, bf16[1088,128]{1,0:T(8,128)(2,1)S(1)}, u32[]{:S(2)}, u32[]{:S(2)}) collective-permute-start(bf16[1088,128]{1,0:T(8,128)(2,1)S(1)} %fusion), channel_id=1, source_target_pairs={{0,2},{1,3},{2,0},{3,1},{4,6},{5,7},{6,4},{7,5},{8,10},{9,11},{10,... | collective-permute-start | bytes 835592 | tf_op jit(solution)/shard_map/ppermute | solution.py:765
  39.1 1.5 %collective-permute-done.15.refs_3_ = bf16[64,512]{1,0:T(8,128)(2,1)S(1)} collective-permute-done((bf16[64,512]{1,0:T(8,128)(2,1)S(1)}, bf16[64,512]{1,0:T(8,128)(2,1)S(1)}, u32[]{:S(2)}, u32[]{:S(2)}) %collective-permute-start.15) | collective-permute-done | bytes 65568 | tf_op jit(solution)/shard_map/ppermute | solution.py:765
  40.8 1.8 %collective-permute-start.16 = (bf16[1040,128]{1,0:T(8,128)(2,1)S(1)}, bf16[1040,128]{1,0:T(8,128)(2,1)S(1)}, u32[]{:S(2)}, u32[]{:S(2)}) collective-permute-start(bf16[1040,128]{1,0:T(8,128)(2,1)S(1)} %fusion.1), channel_id=1, source_target_pairs={{0,2},{1,3},{2,0},{3,1},{4,6},{5,7},{6,4},{7,5},{8,10},{9,11},{10,... | collective-permute-start | bytes 798728 | tf_op jit(solution)/shard_map/ppermute | solution.py:765
  42.6 2.3 %collective-permute-start.21 = (bf16[128,512]{1,0:T(8,128)(2,1)S(1)}, bf16[128,512]{1,0:T(8,128)(2,1)S(1)}, u32[]{:S(2)}, u32[]{:S(2)}) collective-permute-start(bf16[128,512]{1,0:T(8,128)(2,1)S(1)} %total_grads.1.mine_ref), channel_id=1, source_target_pairs={{0,8},{4,12},{8,0},{12,4},{1,9},{5,13},{9,1},{13,5},{2,10},{6,14},... | collective-permute-start | bytes 393224 | tf_op jit(solution)/shard_map/ppermute | solution.py:765
  44.8 1.6 %collective-permute-done.17.last_ref = bf16[1088,128]{1,0:T(8,128)(2,1)S(1)} collective-permute-done((bf16[1088,128]{1,0:T(8,128)(2,1)S(1)}, bf16[1088,128]{1,0:T(8,128)(2,1)S(1)}, u32[]{:S(2)}, u32[]{:S(2)}) %collective-permute-start.17) | collective-permute-done | bytes 278560 | tf_op jit(solution)/shard_map/ppermute | solution.py:765
  46.6 2.5 %collective-permute-start.20 = (bf16[544,128]{1,0:T(8,128)(2,1)S(1)}, bf16[544,128]{1,0:T(8,128)(2,1)S(1)}, u32[]{:S(2)}, u32[]{:S(2)}) collective-permute-start(bf16[544,128]{1,0:T(8,128)(2,1)S(1)} %get-tuple-element.113), channel_id=1, source_target_pairs={{0,8},{4,12},{8,0},{12,4},{1,9},{5,13},{9,1},{13,5},{2,10},{6,14},... | collective-permute-start | bytes 417800 | tf_op jit(solution)/shard_map/ppermute | solution.py:770
  49.5 1.7 %collective-permute-start.19 = (bf16[272,128]{1,0:T(8,128)(2,1)S(1)}, bf16[272,128]{1,0:T(8,128)(2,1)S(1)}, u32[]{:S(2)}, u32[]{:S(2)}) collective-permute-start(bf16[272,128]{1,0:T(8,128)(2,1)S(1)} %get-tuple-element.112), channel_id=1, source_target_pairs={{0,4},{4,8},{8,12},{12,0},{1,5},{5,9},{9,13},{13,1},{2,6},{6,10},{... | collective-permute-start | bytes 208904 | tf_op jit(solution)/shard_map/ppermute | solution.py:770
  51.1 0.7 %own_sum.1 = (bf16[512,128]{1,0:T(8,128)(2,1)}, f32[528,128]{1,0:T(8,128)S(1)}) custom-call(bf16[2,1040,128]{2,1,0:T(8,128)(2,1)S(1)} %get-tuple-element.95.keep_ref, bf16[2,1040,128]{2,1,0:T(8,128)(2,1)S(1)} %collective-permute-done.10.got_ref, bf16[1040,128]{1,0:T(8,128)(2,1)S(1)} %collective-permute-done.16.last_ref), custom_call_target="tpu_custom_call" | custom-call | flops 1 | bytes 1 | tf_op jit(solution)/shard_map/own_sum/pallas_call | solution.py:643
  51.8 2.0 %collective-permute-done.21.got_ref = bf16[128,512]{1,0:T(8,128)(2,1)S(1)} collective-permute-done((bf16[128,512]{1,0:T(8,128)(2,1)S(1)}, bf16[128,512]{1,0:T(8,128)(2,1)S(1)}, u32[]{:S(2)}, u32[]{:S(2)}) %collective-permute-start.21) | collective-permute-done | bytes 131104 | tf_op jit(solution)/shard_map/ppermute | solution.py:765
  53.9 1.2 %collective-permute-start.23 = (bf16[64,512]{1,0:T(8,128)(2,1)S(1)}, bf16[64,512]{1,0:T(8,128)(2,1)S(1)}, u32[]{:S(2)}, u32[]{:S(2)}) collective-permute-start(bf16[64,512]{1,0:T(8,128)(2,1)S(1)} %get-tuple-element.122.refs_2_), channel_id=1, source_target_pairs={{0,16},{16,0},{1,17},{17,1},{2,18},{18,2},{3,19},{19,3},{4,20},{20... | collective-permute-start | bytes 196616 | tf_op jit(solution)/shard_map/ppermute | solution.py:765
  55.1 2.8 %collective-permute-done.18.refs_4_ = bf16[272,128]{1,0:T(8,128)(2,1)S(1)} collective-permute-done((bf16[272,128]{1,0:T(8,128)(2,1)S(1)}, bf16[272,128]{1,0:T(8,128)(2,1)S(1)}, u32[]{:S(2)}, u32[]{:S(2)}) %collective-permute-start.18) | collective-permute-done | bytes 69664 | tf_op jit(solution)/shard_map/ppermute | solution.py:770
  58.0 0.7 %collective-permute-done.22.refs_1_ = bf16[64,512]{1,0:T(8,128)(2,1)S(1)} collective-permute-done((bf16[64,512]{1,0:T(8,128)(2,1)S(1)}, bf16[64,512]{1,0:T(8,128)(2,1)S(1)}, u32[]{:S(2)}, u32[]{:S(2)}) %collective-permute-start.22) | collective-permute-done | bytes 65568 | tf_op jit(solution)/shard_map/ppermute | solution.py:765
  58.7 0.8 %collective-permute-start.24 = (bf16[128,512]{1,0:T(8,128)(2,1)S(1)}, bf16[128,512]{1,0:T(8,128)(2,1)S(1)}, u32[]{:S(2)}, u32[]{:S(2)}) collective-permute-start(bf16[128,512]{1,0:T(8,128)(2,1)S(1)} %get-tuple-element.123.refs_0_), channel_id=1, source_target_pairs={{0,16},{16,0},{1,17},{17,1},{2,18},{18,2},{3,19},{19,3},{4,20},{20... | collective-permute-start | bytes 393224 | tf_op jit(solution)/shard_map/ppermute | solution.py:765
  59.5 2.5 %collective-permute-start.25 = (bf16[128,512]{1,0:T(8,128)(2,1)S(1)}, bf16[128,512]{1,0:T(8,128)(2,1)S(1)}, u32[]{:S(2)}, u32[]{:S(2)}) collective-permute-start(bf16[128,512]{1,0:T(8,128)(2,1)S(1)} %get-tuple-element.125.refs_2_), channel_id=1, source_target_pairs={{0,4},{4,0},{8,12},{12,8},{1,5},{5,1},{9,13},{13,9},{2,6},{6,2},{1... | collective-permute-start | bytes 393224 | tf_op jit(solution)/shard_map/ppermute | solution.py:765
  61.9 1.5 %finish.1 = bf16[512,128]{1,0:T(8,128)(2,1)} custom-call(s32[2,4]{1,0:T(2,128)} %bitcast.16, f32[528,128]{1,0:T(8,128)S(1)} %get-tuple-element.116.refs_1_, f32[512,128]{1,0:T(8,128)S(1)} %get-tuple-element.117.refs_2_, f32[512,128]{1,0:T(8,128)S(1)} %get-tuple-element.118.refs_3_, bf16[272,128]{1,0:T(8,128)(2,1)S(1)} %collective-permute-done.18.refs_4_, ...), custom_call_target="tpu_custom_call" | custom-call | flops 1 | bytes 1 | tf_op jit(solution)/shard_map/finish/pallas_call | solution.py:695
  63.7 1.2 %collective-permute-done.25.refs_3_ = bf16[128,512]{1,0:T(8,128)(2,1)S(1)} collective-permute-done((bf16[128,512]{1,0:T(8,128)(2,1)S(1)}, bf16[128,512]{1,0:T(8,128)(2,1)S(1)}, u32[]{:S(2)}, u32[]{:S(2)}) %collective-permute-start.25) | collective-permute-done | bytes 131104 | tf_op jit(solution)/shard_map/ppermute | solution.py:765
  64.9 1.3 %weight_grads.1 = (f32[512,128]{1,0:T(8,128)}, f32[512,128]{1,0:T(8,128)}, f32[512,128]{1,0:T(8,128)}, f32[128,512]{1,0:T(8,128)}) custom-call(bf16[128,512]{1,0:T(8,128)(2,1)S(1)} %get-tuple-element.123.refs_0_, bf16[128,512]{1,0:T(8,128)(2,1)S(1)} %collective-permute-done.24.refs_1_, bf16[128,512]{1,0:T(8,128)(2,1)S(1)} %get-tuple-element.125.refs_2_, ...), custom_call_target="tpu_custom_call" | custom-call | flops 1 | bytes 1 | tf_op jit(solution)/shard_map/weight_grads/pallas_call | solution.py:749
  (37 shorter events, 6.5 us)
Async XLA Ops:
  1.7 9.2 %collective-permute-start = (bf16[128,512]{1,0:T(8,128)(2,1)S(1)}, bf16[128,512]{1,0:T(8,128)(2,1)S(1)}, u32[]{:S(2)}, u32[]{:S(2)}) collective-permute-start(bf16[128,512]{1,0:T(8,128)(2,1)S(1)} %get-tuple-element.68), channel_id=1, source_target_pairs={{0,4},{1,9},{2,14},{3,11},{4,8},{5,13},{6,2},{7,15},{8,12},{9,1},{... | collective-permute-start | bytes 393224 | tf_op jit(solution)/shard_map/ppermute | solution.py:815
  4.8 8.5 %collective-permute-start.1 = (bf16[128,512]{1,0:T(8,128)(2,1)S(1)}, bf16[128,512]{1,0:T(8,128)(2,1)S(1)}, u32[]{:S(2)}, u32[]{:S(2)}) collective-permute-start(bf16[128,512]{1,0:T(8,128)(2,1)S(1)} %get-tuple-element.71), channel_id=1, source_target_pairs={{0,4},{1,9},{2,14},{3,11},{4,8},{5,13},{6,2},{7,15},{8,12},{9,1},{... | collective-permute-start | bytes 393224 | tf_op jit(solution)/shard_map/ppermute | solution.py:815
  10.9 9.8 %collective-permute-start.6 = (bf16[128,512]{1,0:T(8,128)(2,1)S(1)}, bf16[128,512]{1,0:T(8,128)(2,1)S(1)}, u32[]{:S(2)}, u32[]{:S(2)}) collective-permute-start(bf16[128,512]{1,0:T(8,128)(2,1)S(1)} %collective-permute-done.refs_0_), channel_id=1, source_target_pairs={{0,2},{1,3},{2,0},{3,1},{4,6},{5,7},{6,4},{7,5},{8,10},{9,11},{10,... | collective-permute-start | bytes 393224 | tf_op jit(solution)/shard_map/ppermute | solution.py:765
  13.3 2.4 %collective-permute-start.3 = (bf16[64,512]{1,0:T(8,128)(2,1)S(1)}, bf16[64,512]{1,0:T(8,128)(2,1)S(1)}, u32[]{:S(2)}, u32[]{:S(2)}) collective-permute-start(bf16[64,512]{1,0:T(8,128)(2,1)S(1)} %get-tuple-element.132), channel_id=1, source_target_pairs={{0,1},{1,0},{2,3},{3,2},{4,5},{5,4},{6,7},{7,6},{8,9},{9,8},{10,11... | collective-permute-start | bytes 196616 | tf_op jit(solution)/shard_map/ppermute | solution.py:765
  14.8 1.3 %collective-permute-start.2 = (bf16[64,512]{1,0:T(8,128)(2,1)S(1)}, bf16[64,512]{1,0:T(8,128)(2,1)S(1)}, u32[]{:S(2)}, u32[]{:S(2)}) collective-permute-start(bf16[64,512]{1,0:T(8,128)(2,1)S(1)} %get-tuple-element.133), channel_id=1, source_target_pairs={{0,1},{1,0},{2,3},{3,2},{4,5},{5,4},{6,7},{7,6},{8,9},{9,8},{10,11... | collective-permute-start | bytes 196616 | tf_op jit(solution)/shard_map/ppermute | solution.py:765
  14.9 5.8 %collective-permute-start.7 = (bf16[128,512]{1,0:T(8,128)(2,1)S(1)}, bf16[128,512]{1,0:T(8,128)(2,1)S(1)}, u32[]{:S(2)}, u32[]{:S(2)}) collective-permute-start(bf16[128,512]{1,0:T(8,128)(2,1)S(1)} %collective-permute-done.1.refs_1_), channel_id=1, source_target_pairs={{0,2},{1,3},{2,0},{3,1},{4,6},{5,7},{6,4},{7,5},{8,10},{9,11},{10,... | collective-permute-start | bytes 393224 | tf_op jit(solution)/shard_map/ppermute | solution.py:765
  15.3 1.3 %collective-permute-start.5 = (bf16[64,512]{1,0:T(8,128)(2,1)S(1)}, bf16[64,512]{1,0:T(8,128)(2,1)S(1)}, u32[]{:S(2)}, u32[]{:S(2)}) collective-permute-start(bf16[64,512]{1,0:T(8,128)(2,1)S(1)} %get-tuple-element.130), channel_id=1, source_target_pairs={{0,1},{1,0},{2,3},{3,2},{4,5},{5,4},{6,7},{7,6},{8,9},{9,8},{10,11... | collective-permute-start | bytes 196616 | tf_op jit(solution)/shard_map/ppermute | solution.py:765
  15.7 1.3 %collective-permute-start.4 = (bf16[64,512]{1,0:T(8,128)(2,1)S(1)}, bf16[64,512]{1,0:T(8,128)(2,1)S(1)}, u32[]{:S(2)}, u32[]{:S(2)}) collective-permute-start(bf16[64,512]{1,0:T(8,128)(2,1)S(1)} %get-tuple-element.131), channel_id=1, source_target_pairs={{0,1},{1,0},{2,3},{3,2},{4,5},{5,4},{6,7},{7,6},{8,9},{9,8},{10,11... | collective-permute-start | bytes 196616 | tf_op jit(solution)/shard_map/ppermute | solution.py:765
  20.8 1.3 %collective-permute-start.8 = (bf16[128,512]{1,0:T(8,128)(2,1)S(1)}, bf16[128,512]{1,0:T(8,128)(2,1)S(1)}, u32[]{:S(2)}, u32[]{:S(2)}) collective-permute-start(bf16[128,512]{1,0:T(8,128)(2,1)S(1)} %collective-permute-done.6.refs_5_), channel_id=1, source_target_pairs={{0,1},{1,0},{2,3},{3,2},{4,5},{5,4},{6,7},{7,6},{8,9},{9,8},{10,11... | collective-permute-start | bytes 393224 | tf_op jit(solution)/shard_map/ppermute | solution.py:765
  20.8 1.5 %collective-permute-start.9 = (bf16[128,512]{1,0:T(8,128)(2,1)S(1)}, bf16[128,512]{1,0:T(8,128)(2,1)S(1)}, u32[]{:S(2)}, u32[]{:S(2)}) collective-permute-start(bf16[128,512]{1,0:T(8,128)(2,1)S(1)} %collective-permute-done.7.refs_6_), channel_id=1, source_target_pairs={{0,1},{1,0},{2,3},{3,2},{4,5},{5,4},{6,7},{7,6},{8,9},{9,8},{10,11... | collective-permute-start | bytes 393224 | tf_op jit(solution)/shard_map/ppermute | solution.py:765
  27.4 4.5 %collective-permute-start.12 = (bf16[2,1088,128]{2,1,0:T(8,128)(2,1)S(1)}, bf16[2,1088,128]{2,1,0:T(8,128)(2,1)S(1)}, u32[]{:S(2)}, u32[]{:S(2)}) collective-permute-start(bf16[2,1088,128]{2,1,0:T(8,128)(2,1)S(1)} %get-tuple-element.100), channel_id=1, source_target_pairs={{0,1},{1,0},{2,3},{3,2},{4,5},{5,4},{6,7},{7,6},{8,9},{9,8},{10,11... | collective-permute-start | bytes 1671176 | tf_op jit(solution)/shard_map/ppermute | solution.py:765
  27.8 6.9 %collective-permute-start.11 = (bf16[128,512]{1,0:T(8,128)(2,1)S(1)}, bf16[128,512]{1,0:T(8,128)(2,1)S(1)}, u32[]{:S(2)}, u32[]{:S(2)}) collective-permute-start(bf16[128,512]{1,0:T(8,128)(2,1)S(1)} %get-tuple-element.98), channel_id=1, source_target_pairs={{0,16},{16,0},{1,17},{17,1},{2,18},{18,2},{3,19},{19,3},{4,20},{20... | collective-permute-start | bytes 393224 | tf_op jit(solution)/shard_map/ppermute | solution.py:765
  29.4 5.3 %collective-permute-start.13 = (bf16[128,512]{1,0:T(8,128)(2,1)S(1)}, bf16[128,512]{1,0:T(8,128)(2,1)S(1)}, u32[]{:S(2)}, u32[]{:S(2)}) collective-permute-start(bf16[128,512]{1,0:T(8,128)(2,1)S(1)} %get-tuple-element.103), channel_id=1, source_target_pairs={{0,4},{4,0},{8,12},{12,8},{1,5},{5,1},{9,13},{13,9},{2,6},{6,2},{1... | collective-permute-start | bytes 393224 | tf_op jit(solution)/shard_map/ppermute | solution.py:765
  31.8 8.9 %collective-permute-start.10 = (bf16[2,1040,128]{2,1,0:T(8,128)(2,1)S(1)}, bf16[2,1040,128]{2,1,0:T(8,128)(2,1)S(1)}, u32[]{:S(2)}, u32[]{:S(2)}) collective-permute-start(bf16[2,1040,128]{2,1,0:T(8,128)(2,1)S(1)} %get-tuple-element.96), channel_id=1, source_target_pairs={{0,1},{1,0},{2,3},{3,2},{4,5},{5,4},{6,7},{7,6},{8,9},{9,8},{10,11... | collective-permute-start | bytes 1597448 | tf_op jit(solution)/shard_map/ppermute | solution.py:765
  34.8 4.3 %collective-permute-start.14 = (bf16[64,512]{1,0:T(8,128)(2,1)S(1)}, bf16[64,512]{1,0:T(8,128)(2,1)S(1)}, u32[]{:S(2)}, u32[]{:S(2)}) collective-permute-start(bf16[64,512]{1,0:T(8,128)(2,1)S(1)} %get-tuple-element.106), channel_id=1, source_target_pairs={{0,4},{4,0},{8,12},{12,8},{1,5},{5,1},{9,13},{13,9},{2,6},{6,2},{1... | collective-permute-start | bytes 196616 | tf_op jit(solution)/shard_map/ppermute | solution.py:765
  36.4 4.3 %collective-permute-start.15 = (bf16[64,512]{1,0:T(8,128)(2,1)S(1)}, bf16[64,512]{1,0:T(8,128)(2,1)S(1)}, u32[]{:S(2)}, u32[]{:S(2)}) collective-permute-start(bf16[64,512]{1,0:T(8,128)(2,1)S(1)} %get-tuple-element.108), channel_id=1, source_target_pairs={{0,16},{16,0},{1,17},{17,1},{2,18},{18,2},{3,19},{19,3},{4,20},{20... | collective-permute-start | bytes 196616 | tf_op jit(solution)/shard_map/ppermute | solution.py:765
  36.9 9.6 %collective-permute-start.17 = (bf16[1088,128]{1,0:T(8,128)(2,1)S(1)}, bf16[1088,128]{1,0:T(8,128)(2,1)S(1)}, u32[]{:S(2)}, u32[]{:S(2)}) collective-permute-start(bf16[1088,128]{1,0:T(8,128)(2,1)S(1)} %fusion), channel_id=1, source_target_pairs={{0,2},{1,3},{2,0},{3,1},{4,6},{5,7},{6,4},{7,5},{8,10},{9,11},{10,... | collective-permute-start | bytes 835592 | tf_op jit(solution)/shard_map/ppermute | solution.py:765
  40.8 10.4 %collective-permute-start.16 = (bf16[1040,128]{1,0:T(8,128)(2,1)S(1)}, bf16[1040,128]{1,0:T(8,128)(2,1)S(1)}, u32[]{:S(2)}, u32[]{:S(2)}) collective-permute-start(bf16[1040,128]{1,0:T(8,128)(2,1)S(1)} %fusion.1), channel_id=1, source_target_pairs={{0,2},{1,3},{2,0},{3,1},{4,6},{5,7},{6,4},{7,5},{8,10},{9,11},{10,... | collective-permute-start | bytes 798728 | tf_op jit(solution)/shard_map/ppermute | solution.py:765
  42.6 11.2 %collective-permute-start.21 = (bf16[128,512]{1,0:T(8,128)(2,1)S(1)}, bf16[128,512]{1,0:T(8,128)(2,1)S(1)}, u32[]{:S(2)}, u32[]{:S(2)}) collective-permute-start(bf16[128,512]{1,0:T(8,128)(2,1)S(1)} %total_grads.1.mine_ref), channel_id=1, source_target_pairs={{0,8},{4,12},{8,0},{12,4},{1,9},{5,13},{9,1},{13,5},{2,10},{6,14},... | collective-permute-start | bytes 393224 | tf_op jit(solution)/shard_map/ppermute | solution.py:765
  46.6 12.1 %collective-permute-start.20 = (bf16[544,128]{1,0:T(8,128)(2,1)S(1)}, bf16[544,128]{1,0:T(8,128)(2,1)S(1)}, u32[]{:S(2)}, u32[]{:S(2)}) collective-permute-start(bf16[544,128]{1,0:T(8,128)(2,1)S(1)} %get-tuple-element.113), channel_id=1, source_target_pairs={{0,8},{4,12},{8,0},{12,4},{1,9},{5,13},{9,1},{13,5},{2,10},{6,14},... | collective-permute-start | bytes 417800 | tf_op jit(solution)/shard_map/ppermute | solution.py:770
  49.1 8.8 %collective-permute-start.18 = (bf16[272,128]{1,0:T(8,128)(2,1)S(1)}, bf16[272,128]{1,0:T(8,128)(2,1)S(1)}, u32[]{:S(2)}, u32[]{:S(2)}) collective-permute-start(bf16[272,128]{1,0:T(8,128)(2,1)S(1)} %get-tuple-element.111), channel_id=1, source_target_pairs={{0,12},{4,0},{8,4},{12,8},{1,13},{5,1},{9,5},{13,9},{2,14},{6,2},{... | collective-permute-start | bytes 208904 | tf_op jit(solution)/shard_map/ppermute | solution.py:770
  49.5 8.5 %collective-permute-start.19 = (bf16[272,128]{1,0:T(8,128)(2,1)S(1)}, bf16[272,128]{1,0:T(8,128)(2,1)S(1)}, u32[]{:S(2)}, u32[]{:S(2)}) collective-permute-start(bf16[272,128]{1,0:T(8,128)(2,1)S(1)} %get-tuple-element.112), channel_id=1, source_target_pairs={{0,4},{4,8},{8,12},{12,0},{1,5},{5,9},{9,13},{13,1},{2,6},{6,10},{... | collective-permute-start | bytes 208904 | tf_op jit(solution)/shard_map/ppermute | solution.py:770
  53.8 4.8 %collective-permute-start.22 = (bf16[64,512]{1,0:T(8,128)(2,1)S(1)}, bf16[64,512]{1,0:T(8,128)(2,1)S(1)}, u32[]{:S(2)}, u32[]{:S(2)}) collective-permute-start(bf16[64,512]{1,0:T(8,128)(2,1)S(1)} %get-tuple-element.120.refs_0_), channel_id=1, source_target_pairs={{0,4},{4,0},{8,12},{12,8},{1,5},{5,1},{9,13},{13,9},{2,6},{6,2},{1... | collective-permute-start | bytes 196616 | tf_op jit(solution)/shard_map/ppermute | solution.py:765
  53.9 4.7 %collective-permute-start.23 = (bf16[64,512]{1,0:T(8,128)(2,1)S(1)}, bf16[64,512]{1,0:T(8,128)(2,1)S(1)}, u32[]{:S(2)}, u32[]{:S(2)}) collective-permute-start(bf16[64,512]{1,0:T(8,128)(2,1)S(1)} %get-tuple-element.122.refs_2_), channel_id=1, source_target_pairs={{0,16},{16,0},{1,17},{17,1},{2,18},{18,2},{3,19},{19,3},{4,20},{20... | collective-permute-start | bytes 196616 | tf_op jit(solution)/shard_map/ppermute | solution.py:765
  58.7 5.0 %collective-permute-start.24 = (bf16[128,512]{1,0:T(8,128)(2,1)S(1)}, bf16[128,512]{1,0:T(8,128)(2,1)S(1)}, u32[]{:S(2)}, u32[]{:S(2)}) collective-permute-start(bf16[128,512]{1,0:T(8,128)(2,1)S(1)} %get-tuple-element.123.refs_0_), channel_id=1, source_target_pairs={{0,16},{16,0},{1,17},{17,1},{2,18},{18,2},{3,19},{19,3},{4,20},{20... | collective-permute-start | bytes 393224 | tf_op jit(solution)/shard_map/ppermute | solution.py:765
  59.5 5.4 %collective-permute-start.25 = (bf16[128,512]{1,0:T(8,128)(2,1)S(1)}, bf16[128,512]{1,0:T(8,128)(2,1)S(1)}, u32[]{:S(2)}, u32[]{:S(2)}) collective-permute-start(bf16[128,512]{1,0:T(8,128)(2,1)S(1)} %get-tuple-element.125.refs_2_), channel_id=1, source_target_pairs={{0,4},{4,0},{8,12},{12,8},{1,5},{5,1},{9,13},{13,9},{2,6},{6,2},{1... | collective-permute-start | bytes 393224 | tf_op jit(solution)/shard_map/ppermute | solution.py:765

commit v2 on v1

--- a/solution.py
+++ b/solution.py
@@ -293,6 +293,7 @@
     put_pairs(paired, places, width, k_ref, v_ref, kt_ref, vt_ref)
 
     shrink = 1.0 / math.sqrt(HD)
+    steep = shrink / math.log(2.0)
     near = near_ref.shape[1]
     fetch.wait()
     listed = [[block] + [near_table[block, n] for n in range(near)] for block in range(blocks)]
@@ -300,7 +301,7 @@
     def open_block(block):
         keys = jnp.concatenate([k_ref[block_at(e), :] for e in listed[block]], axis=0)
         values = jnp.concatenate([v_ref[block_at(e), :] for e in listed[block]], axis=0)
-        score_ref[block] = nt(keys, q_ref[block * tall : (block + 1) * tall, :]) * shrink
+        score_ref[block] = nt(keys, q_ref[block * tall : (block + 1) * tall, :])
         prob_ref[block] = nt(values, g_ref[block * tall : (block + 1) * tall, :])
 
     def weigh_block(block):
@@ -311,7 +312,7 @@
             highest = jnp.maximum(highest, rows)
         total, drop = jnp.zeros_like(highest), jnp.zeros_like(highest)
         for span in spans:
-            powers = jnp.exp(score_ref[block, span, :] - highest)
+            powers = jnp.exp2((score_ref[block, span, :] - highest) * steep)
             score_ref[block, span, :] = powers
             total = total + jnp.sum(powers, axis=0, keepdims=True)
             drop = drop + jnp.sum(powers * prob_ref[block, span, :], axis=0, keepdims=True)
@@ -341,9 +342,9 @@
     for block in range(blocks):
         if block + 1 < blocks:
             open_block(block + 1)
-        weigh_block(block)
         if block:
             close_block(block - 1)
+        weigh_block(block)
     close_block(blocks - 1)
 
     ka_ref[own_rows:, :] = jnp.zeros((entries * BLK - own_rows, width), F32)

time: 66.3 us -> 66.2 us (level)
  no operation moved by 1% of the time
where the time goes in v2:
time: 66.2 us; the launch traced here: 66 us
  starting transfers between devices  28.8 us (44%)
  waiting for transfers between devices  23 us (35%)
  Pallas kernels  13.2 us (20%)
  between operations  0.77 us (1%)
    ppermute x21, starting transfers between devices, swap(): lax.ppermute(array, axis, [(i, i ^ bit) for i in range(lax.axis_size(axis...  19.6 us
    ppermute x21, waiting for transfers between devices, swap(): lax.ppermute(array, axis, [(i, i ^ bit) for i in range(lax.axis_size(axis...  15.9 us
    pallas_call x1, Pallas kernels, run_attend(): pl.pallas_call(functools.partial(attend_kernel, cfg), out_shape=[shape((e...  5.03 us
    ppermute x2, starting transfers between devices, body(): lax.ppermute(block, ('dom', 'tensor'), route)  4.65 us
    ppermute x3, starting transfers between devices, shifted(): lax.ppermute(array, axis, [(i, (i + distance) % size) for i in range(size)])  4.57 us
    ppermute x2, waiting for transfers between devices, body(): lax.ppermute(block, ('dom', 'tensor'), route)  4.3 us
    ppermute x3, waiting for transfers between devices, shifted(): lax.ppermute(array, axis, [(i, (i + distance) % size) for i in range(size)])  2.85 us
    pallas_call x1, Pallas kernels, run_own(): pl.pallas_call(own_kernel, out_shape=(shape((rows, feats), BF16), shape((...  2.04 us
  transfers between devices with their start and end apart: 26, of which 17 were waited for; matrix products, arithmetic and copies ran while one was open for 0% of the time, Pallas kernels for 9%

profile of v2, /device:TPU:0, one launch (start us, length us, event | category | flops | bytes accessed | tf_op | source)
XLA Modules:
  0.0 66.0 jit_solution(4225095641524083165)
XLA Ops:
  0.6 1.1 %pick_blocks.1 = (bf16[128,512]{1,0:T(8,128)(2,1)S(1)}, bf16[128,512]{1,0:T(8,128)(2,1)S(1)}) custom-call(s32[2,4]{1,0:T(2,128)} %bitcast.15, bf16[512,512]{1,0:T(8,128)(2,1)} %bitcast.11), custom_call_target="tpu_custom_call" | custom-call | flops 1 | bytes 1 | tf_op jit(solution)/shard_map/pick_blocks/pallas_call | solution.py:88
  1.7 3.1 %collective-permute-start = (bf16[128,512]{1,0:T(8,128)(2,1)S(1)}, bf16[128,512]{1,0:T(8,128)(2,1)S(1)}, u32[]{:S(2)}, u32[]{:S(2)}) collective-permute-start(bf16[128,512]{1,0:T(8,128)(2,1)S(1)} %get-tuple-element.68), channel_id=1, source_target_pairs={{0,4},{1,9},{2,14},{3,11},{4,8},{5,13},{6,2},{7,15},{8,12},{9,1},{... | collective-permute-start | bytes 393224 | tf_op jit(solution)/shard_map/ppermute | solution.py:816
  4.8 1.6 %collective-permute-start.1 = (bf16[128,512]{1,0:T(8,128)(2,1)S(1)}, bf16[128,512]{1,0:T(8,128)(2,1)S(1)}, u32[]{:S(2)}, u32[]{:S(2)}) collective-permute-start(bf16[128,512]{1,0:T(8,128)(2,1)S(1)} %get-tuple-element.71), channel_id=1, source_target_pairs={{0,4},{1,9},{2,14},{3,11},{4,8},{5,13},{6,2},{7,15},{8,12},{9,1},{... | collective-permute-start | bytes 393224 | tf_op jit(solution)/shard_map/ppermute | solution.py:816
  6.4 2.0 %own_rows.1 = (bf16[512,512]{1,0:T(8,128)(2,1)S(1)}, bf16[1024,128]{1,0:T(8,128)(2,1)S(1)}, bf16[1024,128]{1,0:T(8,128)(2,1)S(1)}, bf16[512,128]{1,0:T(8,128)(2,...) custom-call(bf16[512,512]{1,0:T(8,128)(2,1)} %bitcast.12, ...), custom_call_target="tpu_custom_call" | custom-call | flops 1 | bytes 1 | tf_op jit(solution)/shard_map/own_rows/pallas_call | solution.py:182
  8.4 2.5 %collective-permute-done.refs_0_ = bf16[128,512]{1,0:T(8,128)(2,1)S(1)} collective-permute-done((bf16[128,512]{1,0:T(8,128)(2,1)S(1)}, bf16[128,512]{1,0:T(8,128)(2,1)S(1)}, u32[]{:S(2)}, u32[]{:S(2)}) %collective-permute-start) | collective-permute-done | bytes 131104 | tf_op jit(solution)/shard_map/ppermute | solution.py:816
  11.5 1.8 %collective-permute-done.1.refs_1_ = bf16[128,512]{1,0:T(8,128)(2,1)S(1)} collective-permute-done((bf16[128,512]{1,0:T(8,128)(2,1)S(1)}, bf16[128,512]{1,0:T(8,128)(2,1)S(1)}, u32[]{:S(2)}, u32[]{:S(2)}) %collective-permute-start.1) | collective-permute-done | bytes 131104 | tf_op jit(solution)/shard_map/ppermute | solution.py:816
  13.3 1.5 %collective-permute-start.3 = (bf16[64,512]{1,0:T(8,128)(2,1)S(1)}, bf16[64,512]{1,0:T(8,128)(2,1)S(1)}, u32[]{:S(2)}, u32[]{:S(2)}) collective-permute-start(bf16[64,512]{1,0:T(8,128)(2,1)S(1)} %get-tuple-element.132), channel_id=1, source_target_pairs={{0,1},{1,0},{2,3},{3,2},{4,5},{5,4},{6,7},{7,6},{8,9},{9,8},{10,11... | collective-permute-start | bytes 196616 | tf_op jit(solution)/shard_map/ppermute | solution.py:766
  17.4 3.3 %collective-permute-done.7.refs_6_ = bf16[128,512]{1,0:T(8,128)(2,1)S(1)} collective-permute-done((bf16[128,512]{1,0:T(8,128)(2,1)S(1)}, bf16[128,512]{1,0:T(8,128)(2,1)S(1)}, u32[]{:S(2)}, u32[]{:S(2)}) %collective-permute-start.7) | collective-permute-done | bytes 131104 | tf_op jit(solution)/shard_map/ppermute | solution.py:766
  21.3 0.8 %collective-permute-done.8.refs_7_ = bf16[128,512]{1,0:T(8,128)(2,1)S(1)} collective-permute-done((bf16[128,512]{1,0:T(8,128)(2,1)S(1)}, bf16[128,512]{1,0:T(8,128)(2,1)S(1)}, u32[]{:S(2)}, u32[]{:S(2)}) %collective-permute-start.8) | collective-permute-done | bytes 131104 | tf_op jit(solution)/shard_map/ppermute | solution.py:766
  22.3 5.0 %attention.1 = (bf16[1536,256]{1,0:T(8,128)(2,1)S(1)}, bf16[512,128]{1,0:T(8,128)(2,1)S(1)}, bf16[512,128]{1,0:T(8,128)(2,1)S(1)}, bf16[2,1088,128]{2,1,0:T(8,12...) custom-call(s32[4,3]{1,0:T(4,128)} %near_ref.1, ...), custom_call_target="tpu_custom_call" | custom-call | flops 1 | bytes 1 | tf_op jit(solution)/shard_map/attention/pallas_call | solution.py:400
  27.7 1.6 %collective-permute-start.11 = (bf16[128,512]{1,0:T(8,128)(2,1)S(1)}, bf16[128,512]{1,0:T(8,128)(2,1)S(1)}, u32[]{:S(2)}, u32[]{:S(2)}) collective-permute-start(bf16[128,512]{1,0:T(8,128)(2,1)S(1)} %get-tuple-element.98), channel_id=1, source_target_pairs={{0,16},{16,0},{1,17},{17,1},{2,18},{18,2},{3,19},{19,3},{4,20},{20... | collective-permute-start | bytes 393224 | tf_op jit(solution)/shard_map/ppermute | solution.py:766
  29.3 1.5 %collective-permute-start.13 = (bf16[128,512]{1,0:T(8,128)(2,1)S(1)}, bf16[128,512]{1,0:T(8,128)(2,1)S(1)}, u32[]{:S(2)}, u32[]{:S(2)}) collective-permute-start(bf16[128,512]{1,0:T(8,128)(2,1)S(1)} %get-tuple-element.103), channel_id=1, source_target_pairs={{0,4},{4,0},{8,12},{12,8},{1,5},{5,1},{9,13},{13,9},{2,6},{6,2},{1... | collective-permute-start | bytes 393224 | tf_op jit(solution)/shard_map/ppermute | solution.py:766
  30.8 0.9 %own_terms.1 = (bf16[2,1040,128]{2,1,0:T(8,128)(2,1)S(1)}, bf16[2,1040,128]{2,1,0:T(8,128)(2,1)S(1)}) custom-call(bf16[1536,256]{1,0:T(8,128)(2,1)S(1)} %get-tuple-element.90.both_ref, bf16[512,512]{1,0:T(8,128)(2,1)S(1)} %get-tuple-element.69.refs_9_.unit_ref, bf16[512,128]{1,0:T(8,128)(2,1)S(1)} %get-tuple-element.91.dq_ref, ...), custom_call_target="tpu_custom_call" | custom-call | flops 1 | bytes 1 | tf_op jit(solution)/shard_map/own_terms/pallas_call | solution.py:498
  31.9 2.7 %collective-permute-done.13.refs_3_ = bf16[128,512]{1,0:T(8,128)(2,1)S(1)} collective-permute-done((bf16[128,512]{1,0:T(8,128)(2,1)S(1)}, bf16[128,512]{1,0:T(8,128)(2,1)S(1)}, u32[]{:S(2)}, u32[]{:S(2)}) %collective-permute-start.13) | collective-permute-done | bytes 131104 | tf_op jit(solution)/shard_map/ppermute | solution.py:766
  34.7 1.6 %collective-permute-start.14 = (bf16[64,512]{1,0:T(8,128)(2,1)S(1)}, bf16[64,512]{1,0:T(8,128)(2,1)S(1)}, u32[]{:S(2)}, u32[]{:S(2)}) collective-permute-start(bf16[64,512]{1,0:T(8,128)(2,1)S(1)} %get-tuple-element.106), channel_id=1, source_target_pairs={{0,4},{4,0},{8,12},{12,8},{1,5},{5,1},{9,13},{13,9},{2,6},{6,2},{1... | collective-permute-start | bytes 196616 | tf_op jit(solution)/shard_map/ppermute | solution.py:766
  36.8 1.8 %collective-permute-start.17 = (bf16[1088,128]{1,0:T(8,128)(2,1)S(1)}, bf16[1088,128]{1,0:T(8,128)(2,1)S(1)}, u32[]{:S(2)}, u32[]{:S(2)}) collective-permute-start(bf16[1088,128]{1,0:T(8,128)(2,1)S(1)} %fusion), channel_id=1, source_target_pairs={{0,2},{1,3},{2,0},{3,1},{4,6},{5,7},{6,4},{7,5},{8,10},{9,11},{10,... | collective-permute-start | bytes 835592 | tf_op jit(solution)/shard_map/ppermute | solution.py:766
  39.0 1.5 %collective-permute-done.15.refs_3_ = bf16[64,512]{1,0:T(8,128)(2,1)S(1)} collective-permute-done((bf16[64,512]{1,0:T(8,128)(2,1)S(1)}, bf16[64,512]{1,0:T(8,128)(2,1)S(1)}, u32[]{:S(2)}, u32[]{:S(2)}) %collective-permute-start.15) | collective-permute-done | bytes 65568 | tf_op jit(solution)/shard_map/ppermute | solution.py:766
  40.6 1.8 %collective-permute-start.16 = (bf16[1040,128]{1,0:T(8,128)(2,1)S(1)}, bf16[1040,128]{1,0:T(8,128)(2,1)S(1)}, u32[]{:S(2)}, u32[]{:S(2)}) collective-permute-start(bf16[1040,128]{1,0:T(8,128)(2,1)S(1)} %fusion.1), channel_id=1, source_target_pairs={{0,2},{1,3},{2,0},{3,1},{4,6},{5,7},{6,4},{7,5},{8,10},{9,11},{10,... | collective-permute-start | bytes 798728 | tf_op jit(solution)/shard_map/ppermute | solution.py:766
  42.5 2.3 %collective-permute-start.21 = (bf16[128,512]{1,0:T(8,128)(2,1)S(1)}, bf16[128,512]{1,0:T(8,128)(2,1)S(1)}, u32[]{:S(2)}, u32[]{:S(2)}) collective-permute-start(bf16[128,512]{1,0:T(8,128)(2,1)S(1)} %total_grads.1.mine_ref), channel_id=1, source_target_pairs={{0,8},{4,12},{8,0},{12,4},{1,9},{5,13},{9,1},{13,5},{2,10},{6,14},... | collective-permute-start | bytes 393224 | tf_op jit(solution)/shard_map/ppermute | solution.py:766
  44.7 1.6 %collective-permute-done.17.last_ref = bf16[1088,128]{1,0:T(8,128)(2,1)S(1)} collective-permute-done((bf16[1088,128]{1,0:T(8,128)(2,1)S(1)}, bf16[1088,128]{1,0:T(8,128)(2,1)S(1)}, u32[]{:S(2)}, u32[]{:S(2)}) %collective-permute-start.17) | collective-permute-done | bytes 278560 | tf_op jit(solution)/shard_map/ppermute | solution.py:766
  46.5 2.5 %collective-permute-start.20 = (bf16[544,128]{1,0:T(8,128)(2,1)S(1)}, bf16[544,128]{1,0:T(8,128)(2,1)S(1)}, u32[]{:S(2)}, u32[]{:S(2)}) collective-permute-start(bf16[544,128]{1,0:T(8,128)(2,1)S(1)} %get-tuple-element.113), channel_id=1, source_target_pairs={{0,8},{4,12},{8,0},{12,4},{1,9},{5,13},{9,1},{13,5},{2,10},{6,14},... | collective-permute-start | bytes 417800 | tf_op jit(solution)/shard_map/ppermute | solution.py:771
  49.4 1.7 %collective-permute-start.19 = (bf16[272,128]{1,0:T(8,128)(2,1)S(1)}, bf16[272,128]{1,0:T(8,128)(2,1)S(1)}, u32[]{:S(2)}, u32[]{:S(2)}) collective-permute-start(bf16[272,128]{1,0:T(8,128)(2,1)S(1)} %get-tuple-element.112), channel_id=1, source_target_pairs={{0,4},{4,8},{8,12},{12,0},{1,5},{5,9},{9,13},{13,1},{2,6},{6,10},{... | collective-permute-start | bytes 208904 | tf_op jit(solution)/shard_map/ppermute | solution.py:771
  51.0 0.7 %own_sum.1 = (bf16[512,128]{1,0:T(8,128)(2,1)}, f32[528,128]{1,0:T(8,128)S(1)}) custom-call(bf16[2,1040,128]{2,1,0:T(8,128)(2,1)S(1)} %get-tuple-element.95.keep_ref, bf16[2,1040,128]{2,1,0:T(8,128)(2,1)S(1)} %collective-permute-done.10.got_ref, bf16[1040,128]{1,0:T(8,128)(2,1)S(1)} %collective-permute-done.16.last_ref), custom_call_target="tpu_custom_call" | custom-call | flops 1 | bytes 1 | tf_op jit(solution)/shard_map/own_sum/pallas_call | solution.py:644
  51.7 2.0 %collective-permute-done.21.got_ref = bf16[128,512]{1,0:T(8,128)(2,1)S(1)} collective-permute-done((bf16[128,512]{1,0:T(8,128)(2,1)S(1)}, bf16[128,512]{1,0:T(8,128)(2,1)S(1)}, u32[]{:S(2)}, u32[]{:S(2)}) %collective-permute-start.21) | collective-permute-done | bytes 131104 | tf_op jit(solution)/shard_map/ppermute | solution.py:766
  53.8 1.2 %collective-permute-start.23 = (bf16[64,512]{1,0:T(8,128)(2,1)S(1)}, bf16[64,512]{1,0:T(8,128)(2,1)S(1)}, u32[]{:S(2)}, u32[]{:S(2)}) collective-permute-start(bf16[64,512]{1,0:T(8,128)(2,1)S(1)} %get-tuple-element.122.refs_2_), channel_id=1, source_target_pairs={{0,16},{16,0},{1,17},{17,1},{2,18},{18,2},{3,19},{19,3},{4,20},{20... | collective-permute-start | bytes 196616 | tf_op jit(solution)/shard_map/ppermute | solution.py:766
  55.0 2.8 %collective-permute-done.18.refs_4_ = bf16[272,128]{1,0:T(8,128)(2,1)S(1)} collective-permute-done((bf16[272,128]{1,0:T(8,128)(2,1)S(1)}, bf16[272,128]{1,0:T(8,128)(2,1)S(1)}, u32[]{:S(2)}, u32[]{:S(2)}) %collective-permute-start.18) | collective-permute-done | bytes 69664 | tf_op jit(solution)/shard_map/ppermute | solution.py:771
  57.8 0.7 %collective-permute-done.22.refs_1_ = bf16[64,512]{1,0:T(8,128)(2,1)S(1)} collective-permute-done((bf16[64,512]{1,0:T(8,128)(2,1)S(1)}, bf16[64,512]{1,0:T(8,128)(2,1)S(1)}, u32[]{:S(2)}, u32[]{:S(2)}) %collective-permute-start.22) | collective-permute-done | bytes 65568 | tf_op jit(solution)/shard_map/ppermute | solution.py:766
  58.6 0.8 %collective-permute-start.24 = (bf16[128,512]{1,0:T(8,128)(2,1)S(1)}, bf16[128,512]{1,0:T(8,128)(2,1)S(1)}, u32[]{:S(2)}, u32[]{:S(2)}) collective-permute-start(bf16[128,512]{1,0:T(8,128)(2,1)S(1)} %get-tuple-element.123.refs_0_), channel_id=1, source_target_pairs={{0,16},{16,0},{1,17},{17,1},{2,18},{18,2},{3,19},{19,3},{4,20},{20... | collective-permute-start | bytes 393224 | tf_op jit(solution)/shard_map/ppermute | solution.py:766
  59.4 2.5 %collective-permute-start.25 = (bf16[128,512]{1,0:T(8,128)(2,1)S(1)}, bf16[128,512]{1,0:T(8,128)(2,1)S(1)}, u32[]{:S(2)}, u32[]{:S(2)}) collective-permute-start(bf16[128,512]{1,0:T(8,128)(2,1)S(1)} %get-tuple-element.125.refs_2_), channel_id=1, source_target_pairs={{0,4},{4,0},{8,12},{12,8},{1,5},{5,1},{9,13},{13,9},{2,6},{6,2},{1... | collective-permute-start | bytes 393224 | tf_op jit(solution)/shard_map/ppermute | solution.py:766
  61.8 1.5 %finish.1 = bf16[512,128]{1,0:T(8,128)(2,1)} custom-call(s32[2,4]{1,0:T(2,128)} %bitcast.16, f32[528,128]{1,0:T(8,128)S(1)} %get-tuple-element.116.refs_1_, f32[512,128]{1,0:T(8,128)S(1)} %get-tuple-element.117.refs_2_, f32[512,128]{1,0:T(8,128)S(1)} %get-tuple-element.118.refs_3_, bf16[272,128]{1,0:T(8,128)(2,1)S(1)} %collective-permute-done.18.refs_4_, ...), custom_call_target="tpu_custom_call" | custom-call | flops 1 | bytes 1 | tf_op jit(solution)/shard_map/finish/pallas_call | solution.py:696
  63.6 1.2 %collective-permute-done.25.refs_3_ = bf16[128,512]{1,0:T(8,128)(2,1)S(1)} collective-permute-done((bf16[128,512]{1,0:T(8,128)(2,1)S(1)}, bf16[128,512]{1,0:T(8,128)(2,1)S(1)}, u32[]{:S(2)}, u32[]{:S(2)}) %collective-permute-start.25) | collective-permute-done | bytes 131104 | tf_op jit(solution)/shard_map/ppermute | solution.py:766
  64.8 1.3 %weight_grads.1 = (f32[512,128]{1,0:T(8,128)}, f32[512,128]{1,0:T(8,128)}, f32[512,128]{1,0:T(8,128)}, f32[128,512]{1,0:T(8,128)}) custom-call(bf16[128,512]{1,0:T(8,128)(2,1)S(1)} %get-tuple-element.123.refs_0_, bf16[128,512]{1,0:T(8,128)(2,1)S(1)} %collective-permute-done.24.refs_1_, bf16[128,512]{1,0:T(8,128)(2,1)S(1)} %get-tuple-element.125.refs_2_, ...), custom_call_target="tpu_custom_call" | custom-call | flops 1 | bytes 1 | tf_op jit(solution)/shard_map/weight_grads/pallas_call | solution.py:750
  (37 shorter events, 6.4 us)
Async XLA Ops:
  1.7 9.2 %collective-permute-start = (bf16[128,512]{1,0:T(8,128)(2,1)S(1)}, bf16[128,512]{1,0:T(8,128)(2,1)S(1)}, u32[]{:S(2)}, u32[]{:S(2)}) collective-permute-start(bf16[128,512]{1,0:T(8,128)(2,1)S(1)} %get-tuple-element.68), channel_id=1, source_target_pairs={{0,4},{1,9},{2,14},{3,11},{4,8},{5,13},{6,2},{7,15},{8,12},{9,1},{... | collective-permute-start | bytes 393224 | tf_op jit(solution)/shard_map/ppermute | solution.py:816
  4.8 8.5 %collective-permute-start.1 = (bf16[128,512]{1,0:T(8,128)(2,1)S(1)}, bf16[128,512]{1,0:T(8,128)(2,1)S(1)}, u32[]{:S(2)}, u32[]{:S(2)}) collective-permute-start(bf16[128,512]{1,0:T(8,128)(2,1)S(1)} %get-tuple-element.71), channel_id=1, source_target_pairs={{0,4},{1,9},{2,14},{3,11},{4,8},{5,13},{6,2},{7,15},{8,12},{9,1},{... | collective-permute-start | bytes 393224 | tf_op jit(solution)/shard_map/ppermute | solution.py:816
  10.9 9.8 %collective-permute-start.6 = (bf16[128,512]{1,0:T(8,128)(2,1)S(1)}, bf16[128,512]{1,0:T(8,128)(2,1)S(1)}, u32[]{:S(2)}, u32[]{:S(2)}) collective-permute-start(bf16[128,512]{1,0:T(8,128)(2,1)S(1)} %collective-permute-done.refs_0_), channel_id=1, source_target_pairs={{0,2},{1,3},{2,0},{3,1},{4,6},{5,7},{6,4},{7,5},{8,10},{9,11},{10,... | collective-permute-start | bytes 393224 | tf_op jit(solution)/shard_map/ppermute | solution.py:766
  13.3 2.4 %collective-permute-start.3 = (bf16[64,512]{1,0:T(8,128)(2,1)S(1)}, bf16[64,512]{1,0:T(8,128)(2,1)S(1)}, u32[]{:S(2)}, u32[]{:S(2)}) collective-permute-start(bf16[64,512]{1,0:T(8,128)(2,1)S(1)} %get-tuple-element.132), channel_id=1, source_target_pairs={{0,1},{1,0},{2,3},{3,2},{4,5},{5,4},{6,7},{7,6},{8,9},{9,8},{10,11... | collective-permute-start | bytes 196616 | tf_op jit(solution)/shard_map/ppermute | solution.py:766
  14.8 1.3 %collective-permute-start.2 = (bf16[64,512]{1,0:T(8,128)(2,1)S(1)}, bf16[64,512]{1,0:T(8,128)(2,1)S(1)}, u32[]{:S(2)}, u32[]{:S(2)}) collective-permute-start(bf16[64,512]{1,0:T(8,128)(2,1)S(1)} %get-tuple-element.133), channel_id=1, source_target_pairs={{0,1},{1,0},{2,3},{3,2},{4,5},{5,4},{6,7},{7,6},{8,9},{9,8},{10,11... | collective-permute-start | bytes 196616 | tf_op jit(solution)/shard_map/ppermute | solution.py:766
  14.9 5.8 %collective-permute-start.7 = (bf16[128,512]{1,0:T(8,128)(2,1)S(1)}, bf16[128,512]{1,0:T(8,128)(2,1)S(1)}, u32[]{:S(2)}, u32[]{:S(2)}) collective-permute-start(bf16[128,512]{1,0:T(8,128)(2,1)S(1)} %collective-permute-done.1.refs_1_), channel_id=1, source_target_pairs={{0,2},{1,3},{2,0},{3,1},{4,6},{5,7},{6,4},{7,5},{8,10},{9,11},{10,... | collective-permute-start | bytes 393224 | tf_op jit(solution)/shard_map/ppermute | solution.py:766
  15.3 1.3 %collective-permute-start.5 = (bf16[64,512]{1,0:T(8,128)(2,1)S(1)}, bf16[64,512]{1,0:T(8,128)(2,1)S(1)}, u32[]{:S(2)}, u32[]{:S(2)}) collective-permute-start(bf16[64,512]{1,0:T(8,128)(2,1)S(1)} %get-tuple-element.130), channel_id=1, source_target_pairs={{0,1},{1,0},{2,3},{3,2},{4,5},{5,4},{6,7},{7,6},{8,9},{9,8},{10,11... | collective-permute-start | bytes 196616 | tf_op jit(solution)/shard_map/ppermute | solution.py:766
  15.7 1.3 %collective-permute-start.4 = (bf16[64,512]{1,0:T(8,128)(2,1)S(1)}, bf16[64,512]{1,0:T(8,128)(2,1)S(1)}, u32[]{:S(2)}, u32[]{:S(2)}) collective-permute-start(bf16[64,512]{1,0:T(8,128)(2,1)S(1)} %get-tuple-element.131), channel_id=1, source_target_pairs={{0,1},{1,0},{2,3},{3,2},{4,5},{5,4},{6,7},{7,6},{8,9},{9,8},{10,11... | collective-permute-start | bytes 196616 | tf_op jit(solution)/shard_map/ppermute | solution.py:766
  20.8 1.3 %collective-permute-start.8 = (bf16[128,512]{1,0:T(8,128)(2,1)S(1)}, bf16[128,512]{1,0:T(8,128)(2,1)S(1)}, u32[]{:S(2)}, u32[]{:S(2)}) collective-permute-start(bf16[128,512]{1,0:T(8,128)(2,1)S(1)} %collective-permute-done.6.refs_5_), channel_id=1, source_target_pairs={{0,1},{1,0},{2,3},{3,2},{4,5},{5,4},{6,7},{7,6},{8,9},{9,8},{10,11... | collective-permute-start | bytes 393224 | tf_op jit(solution)/shard_map/ppermute | solution.py:766
  20.8 1.5 %collective-permute-start.9 = (bf16[128,512]{1,0:T(8,128)(2,1)S(1)}, bf16[128,512]{1,0:T(8,128)(2,1)S(1)}, u32[]{:S(2)}, u32[]{:S(2)}) collective-permute-start(bf16[128,512]{1,0:T(8,128)(2,1)S(1)} %collective-permute-done.7.refs_6_), channel_id=1, source_target_pairs={{0,1},{1,0},{2,3},{3,2},{4,5},{5,4},{6,7},{7,6},{8,9},{9,8},{10,11... | collective-permute-start | bytes 393224 | tf_op jit(solution)/shard_map/ppermute | solution.py:766
  27.3 4.5 %collective-permute-start.12 = (bf16[2,1088,128]{2,1,0:T(8,128)(2,1)S(1)}, bf16[2,1088,128]{2,1,0:T(8,128)(2,1)S(1)}, u32[]{:S(2)}, u32[]{:S(2)}) collective-permute-start(bf16[2,1088,128]{2,1,0:T(8,128)(2,1)S(1)} %get-tuple-element.100), channel_id=1, source_target_pairs={{0,1},{1,0},{2,3},{3,2},{4,5},{5,4},{6,7},{7,6},{8,9},{9,8},{10,11... | collective-permute-start | bytes 1671176 | tf_op jit(solution)/shard_map/ppermute | solution.py:766
  27.7 6.9 %collective-permute-start.11 = (bf16[128,512]{1,0:T(8,128)(2,1)S(1)}, bf16[128,512]{1,0:T(8,128)(2,1)S(1)}, u32[]{:S(2)}, u32[]{:S(2)}) collective-permute-start(bf16[128,512]{1,0:T(8,128)(2,1)S(1)} %get-tuple-element.98), channel_id=1, source_target_pairs={{0,16},{16,0},{1,17},{17,1},{2,18},{18,2},{3,19},{19,3},{4,20},{20... | collective-permute-start | bytes 393224 | tf_op jit(solution)/shard_map/ppermute | solution.py:766
  29.3 5.3 %collective-permute-start.13 = (bf16[128,512]{1,0:T(8,128)(2,1)S(1)}, bf16[128,512]{1,0:T(8,128)(2,1)S(1)}, u32[]{:S(2)}, u32[]{:S(2)}) collective-permute-start(bf16[128,512]{1,0:T(8,128)(2,1)S(1)} %get-tuple-element.103), channel_id=1, source_target_pairs={{0,4},{4,0},{8,12},{12,8},{1,5},{5,1},{9,13},{13,9},{2,6},{6,2},{1... | collective-permute-start | bytes 393224 | tf_op jit(solution)/shard_map/ppermute | solution.py:766
  31.7 8.9 %collective-permute-start.10 = (bf16[2,1040,128]{2,1,0:T(8,128)(2,1)S(1)}, bf16[2,1040,128]{2,1,0:T(8,128)(2,1)S(1)}, u32[]{:S(2)}, u32[]{:S(2)}) collective-permute-start(bf16[2,1040,128]{2,1,0:T(8,128)(2,1)S(1)} %get-tuple-element.96), channel_id=1, source_target_pairs={{0,1},{1,0},{2,3},{3,2},{4,5},{5,4},{6,7},{7,6},{8,9},{9,8},{10,11... | collective-permute-start | bytes 1597448 | tf_op jit(solution)/shard_map/ppermute | solution.py:766
  34.7 4.3 %collective-permute-start.14 = (bf16[64,512]{1,0:T(8,128)(2,1)S(1)}, bf16[64,512]{1,0:T(8,128)(2,1)S(1)}, u32[]{:S(2)}, u32[]{:S(2)}) collective-permute-start(bf16[64,512]{1,0:T(8,128)(2,1)S(1)} %get-tuple-element.106), channel_id=1, source_target_pairs={{0,4},{4,0},{8,12},{12,8},{1,5},{5,1},{9,13},{13,9},{2,6},{6,2},{1... | collective-permute-start | bytes 196616 | tf_op jit(solution)/shard_map/ppermute | solution.py:766
  36.3 4.3 %collective-permute-start.15 = (bf16[64,512]{1,0:T(8,128)(2,1)S(1)}, bf16[64,512]{1,0:T(8,128)(2,1)S(1)}, u32[]{:S(2)}, u32[]{:S(2)}) collective-permute-start(bf16[64,512]{1,0:T(8,128)(2,1)S(1)} %get-tuple-element.108), channel_id=1, source_target_pairs={{0,16},{16,0},{1,17},{17,1},{2,18},{18,2},{3,19},{19,3},{4,20},{20... | collective-permute-start | bytes 196616 | tf_op jit(solution)/shard_map/ppermute | solution.py:766
  36.8 9.6 %collective-permute-start.17 = (bf16[1088,128]{1,0:T(8,128)(2,1)S(1)}, bf16[1088,128]{1,0:T(8,128)(2,1)S(1)}, u32[]{:S(2)}, u32[]{:S(2)}) collective-permute-start(bf16[1088,128]{1,0:T(8,128)(2,1)S(1)} %fusion), channel_id=1, source_target_pairs={{0,2},{1,3},{2,0},{3,1},{4,6},{5,7},{6,4},{7,5},{8,10},{9,11},{10,... | collective-permute-start | bytes 835592 | tf_op jit(solution)/shard_map/ppermute | solution.py:766
  40.6 10.4 %collective-permute-start.16 = (bf16[1040,128]{1,0:T(8,128)(2,1)S(1)}, bf16[1040,128]{1,0:T(8,128)(2,1)S(1)}, u32[]{:S(2)}, u32[]{:S(2)}) collective-permute-start(bf16[1040,128]{1,0:T(8,128)(2,1)S(1)} %fusion.1), channel_id=1, source_target_pairs={{0,2},{1,3},{2,0},{3,1},{4,6},{5,7},{6,4},{7,5},{8,10},{9,11},{10,... | collective-permute-start | bytes 798728 | tf_op jit(solution)/shard_map/ppermute | solution.py:766
  42.5 11.3 %collective-permute-start.21 = (bf16[128,512]{1,0:T(8,128)(2,1)S(1)}, bf16[128,512]{1,0:T(8,128)(2,1)S(1)}, u32[]{:S(2)}, u32[]{:S(2)}) collective-permute-start(bf16[128,512]{1,0:T(8,128)(2,1)S(1)} %total_grads.1.mine_ref), channel_id=1, source_target_pairs={{0,8},{4,12},{8,0},{12,4},{1,9},{5,13},{9,1},{13,5},{2,10},{6,14},... | collective-permute-start | bytes 393224 | tf_op jit(solution)/shard_map/ppermute | solution.py:766
  46.5 12.1 %collective-permute-start.20 = (bf16[544,128]{1,0:T(8,128)(2,1)S(1)}, bf16[544,128]{1,0:T(8,128)(2,1)S(1)}, u32[]{:S(2)}, u32[]{:S(2)}) collective-permute-start(bf16[544,128]{1,0:T(8,128)(2,1)S(1)} %get-tuple-element.113), channel_id=1, source_target_pairs={{0,8},{4,12},{8,0},{12,4},{1,9},{5,13},{9,1},{13,5},{2,10},{6,14},... | collective-permute-start | bytes 417800 | tf_op jit(solution)/shard_map/ppermute | solution.py:771
  49.0 8.8 %collective-permute-start.18 = (bf16[272,128]{1,0:T(8,128)(2,1)S(1)}, bf16[272,128]{1,0:T(8,128)(2,1)S(1)}, u32[]{:S(2)}, u32[]{:S(2)}) collective-permute-start(bf16[272,128]{1,0:T(8,128)(2,1)S(1)} %get-tuple-element.111), channel_id=1, source_target_pairs={{0,12},{4,0},{8,4},{12,8},{1,13},{5,1},{9,5},{13,9},{2,14},{6,2},{... | collective-permute-start | bytes 208904 | tf_op jit(solution)/shard_map/ppermute | solution.py:771
  49.4 8.5 %collective-permute-start.19 = (bf16[272,128]{1,0:T(8,128)(2,1)S(1)}, bf16[272,128]{1,0:T(8,128)(2,1)S(1)}, u32[]{:S(2)}, u32[]{:S(2)}) collective-permute-start(bf16[272,128]{1,0:T(8,128)(2,1)S(1)} %get-tuple-element.112), channel_id=1, source_target_pairs={{0,4},{4,8},{8,12},{12,0},{1,5},{5,9},{9,13},{13,1},{2,6},{6,10},{... | collective-permute-start | bytes 208904 | tf_op jit(solution)/shard_map/ppermute | solution.py:771
  53.7 4.8 %collective-permute-start.22 = (bf16[64,512]{1,0:T(8,128)(2,1)S(1)}, bf16[64,512]{1,0:T(8,128)(2,1)S(1)}, u32[]{:S(2)}, u32[]{:S(2)}) collective-permute-start(bf16[64,512]{1,0:T(8,128)(2,1)S(1)} %get-tuple-element.120.refs_0_), channel_id=1, source_target_pairs={{0,4},{4,0},{8,12},{12,8},{1,5},{5,1},{9,13},{13,9},{2,6},{6,2},{1... | collective-permute-start | bytes 196616 | tf_op jit(solution)/shard_map/ppermute | solution.py:766
  53.8 4.7 %collective-permute-start.23 = (bf16[64,512]{1,0:T(8,128)(2,1)S(1)}, bf16[64,512]{1,0:T(8,128)(2,1)S(1)}, u32[]{:S(2)}, u32[]{:S(2)}) collective-permute-start(bf16[64,512]{1,0:T(8,128)(2,1)S(1)} %get-tuple-element.122.refs_2_), channel_id=1, source_target_pairs={{0,16},{16,0},{1,17},{17,1},{2,18},{18,2},{3,19},{19,3},{4,20},{20... | collective-permute-start | bytes 196616 | tf_op jit(solution)/shard_map/ppermute | solution.py:766
  58.6 5.0 %collective-permute-start.24 = (bf16[128,512]{1,0:T(8,128)(2,1)S(1)}, bf16[128,512]{1,0:T(8,128)(2,1)S(1)}, u32[]{:S(2)}, u32[]{:S(2)}) collective-permute-start(bf16[128,512]{1,0:T(8,128)(2,1)S(1)} %get-tuple-element.123.refs_0_), channel_id=1, source_target_pairs={{0,16},{16,0},{1,17},{17,1},{2,18},{18,2},{3,19},{19,3},{4,20},{20... | collective-permute-start | bytes 393224 | tf_op jit(solution)/shard_map/ppermute | solution.py:766
  59.4 5.4 %collective-permute-start.25 = (bf16[128,512]{1,0:T(8,128)(2,1)S(1)}, bf16[128,512]{1,0:T(8,128)(2,1)S(1)}, u32[]{:S(2)}, u32[]{:S(2)}) collective-permute-start(bf16[128,512]{1,0:T(8,128)(2,1)S(1)} %get-tuple-element.125.refs_2_), channel_id=1, source_target_pairs={{0,4},{4,0},{8,12},{12,8},{1,5},{5,1},{9,13},{13,9},{2,6},{6,2},{1... | collective-permute-start | bytes 393224 | tf_op jit(solution)/shard_map/ppermute | solution.py:766
